TPU v7x, 32 devices: a whole 2x2x4 slice. The times are simulated.
32 devices in a mesh: groups: 2 (over x), inst: 8 (over z, y), tp: 2 (over core).
Axes of the slice: x: 2, y: 2, z: 4, core: 2. Of those that a mesh axis runs over, the one named last changes fastest.
Arguments:
- request_dest: int32 [16, 8], P(('groups', 'inst')), parts along dimension 0, may hold values from 0 to 7, as said below
- request_slot: int32 [16, 8], P(('groups', 'inst')), parts along dimension 0, may hold values from 0 to 7, as said below
- page_len: int32 [16, 8], P(('groups', 'inst')), parts along dimension 0, may hold values from 1 to 32
- page_rows: bfloat16 [16, 8, 32, 2, 8, 128], P(('groups', 'inst'), None, None, None, 'tp'), parts along dimension 0, may hold values from -6 to 6
- kv_cache: bfloat16 [16, 1024, 2, 8, 128], P(('groups', 'inst'), None, None, 'tp'), parts along dimension 0, may hold values from -6 to 6
- decode_cache: bfloat16 [16, 64, 2, 8, 128], P(('groups', 'inst'), None, None, 'tp'), parts along dimension 0, may hold values from -6 to 6
- prefix_len: int32 [16], P(('groups', 'inst')), parts along dimension 0, may hold values from 1 to 1024
- cached_len: int32 [16, 8], P(('groups', 'inst')), parts along dimension 0, may hold values from 0 to 8
- queries: bfloat16 [16, 272, 64, 128], P(('groups', 'inst'), None, 'tp'), parts along dimension 0
- fresh_kv: bfloat16 [16, 272, 2, 8, 128], P(('groups', 'inst'), None, None, 'tp'), parts along dimension 0, may hold values from -6 to 6
Outputs:
- attention: bfloat16 [16, 272, 64, 128], P(('groups', 'inst'), None, 'tp'), parts along dimension 0
There are 2 independent parts, one for each index of `groups`. A program takes and returns all parts, laid end to end along the dimension named above; each array names one. Nothing has to cross between parts.
Inputs may be any that keep to these rules, and one draw needn't show every extreme that they name: `request_dest`: each instance's requests name 4 distinct instances, 2 requests each; every instance is named by exactly 8 requests in all. `request_slot`: the requests that reach one instance have distinct slots, so every slot of every instance is taken.
All inputs are finite; a program needn't handle non-finite values.
Results may differ from a plain program's by a relative error of at most 0.0045.
Values may be sent and summed in bfloat16 or wider, within the bound.
No kernel may reach another device: no remote copies, remote signals or barrier semaphores. Data moves between devices by JAX's collectives and lax.ppermute only.
A program may use at most 192 MiB of HBM per device.

v0:
```python
import math

import jax
import jax.numpy as jnp
from jax import lax
from jax.sharding import PartitionSpec as P

PAIR = 2


NEG = -1e30


def merge_block(carried, scores, allowed, values, einsum_form):
    running_max, weight_sum, summed = carried
    masked = jnp.where(allowed, scores, NEG)
    new_max = jnp.maximum(running_max, jnp.max(masked, axis=-1))
    shrink = jnp.exp(running_max - new_max)
    weights = jnp.where(allowed, jnp.exp(masked - new_max[..., None]), 0.0)
    weight_sum = weight_sum * shrink + jnp.sum(weights, axis=-1)
    summed = summed * shrink[..., None] + jnp.einsum(
        einsum_form, weights.astype(jnp.bfloat16), values, preferred_element_type=jnp.float32
    )
    return (new_max, weight_sum, summed)


def empty_state(lead_shape, head_width):
    return (
        jnp.full(lead_shape, NEG, jnp.float32),
        jnp.zeros(lead_shape, jnp.float32),
        jnp.zeros(lead_shape + (head_width,), jnp.float32),
    )


def slot_mask(cached, page_count, cache_depth, page_depth):
    slot_count = cached.shape[0]
    own_ok = jnp.broadcast_to(
        jnp.arange(cache_depth, dtype=jnp.int32)[None, None, :] < cached[None, :, None],
        (2, slot_count, cache_depth),
    )
    page_ok = jnp.broadcast_to(
        jnp.arange(page_depth, dtype=jnp.int32)[None, None, :] < page_count[None, :, None],
        (2, slot_count, page_depth),
    )
    steps_ok = jnp.broadcast_to(
        jnp.arange(2, dtype=jnp.int32)[None, None, :]
        <= jnp.arange(2, dtype=jnp.int32)[:, None, None],
        (2, slot_count, 2),
    )
    return jnp.concatenate([own_ok, page_ok, steps_ok], -1)


def tail_attention(query_rows, cache_rows, fresh_rows, prefix):
    tail_count, head_count, head_width = query_rows.shape
    kv_count = cache_rows.shape[2]
    grouped = query_rows.reshape(tail_count, kv_count, head_count // kv_count, head_width)
    scaling = 1.0 / math.sqrt(head_width)
    cache_depth = cache_rows.shape[0]
    block_rows = min(512, cache_depth)

    def visit_block(blk_index, carried):
        begin_row = blk_index * block_rows
        block_kv = lax.dynamic_slice_in_dim(cache_rows, begin_row, block_rows, 0)
        scores = (
            jnp.einsum(
                "tkgd,jkd->kgtj", grouped, block_kv[:, 0], preferred_element_type=jnp.float32
            )
            * scaling
        )
        allowed = (begin_row + jnp.arange(block_rows, dtype=jnp.int32))[
            None, None, None, :
        ] < prefix
        return merge_block(carried, scores, allowed, block_kv[:, 1], "kgtj,jkd->kgtd")

    visits = cache_depth // block_rows
    carried = lax.fori_loop(
        0,
        visits,
        visit_block,
        empty_state((kv_count, head_count // kv_count, tail_count), head_width),
    )
    scores = (
        jnp.einsum("tkgd,jkd->kgtj", grouped, fresh_rows[:, 0], preferred_element_type=jnp.float32)
        * scaling
    )
    positions = jnp.arange(tail_count, dtype=jnp.int32)
    allowed = (positions[None, :] <= positions[:, None])[None, None]
    running_max, weight_sum, summed = merge_block(
        carried, scores, allowed, fresh_rows[:, 1], "kgtj,jkd->kgtd"
    )
    mixed = summed / weight_sum[..., None]
    return (
        jnp.transpose(mixed, (2, 0, 1, 3))
        .reshape(tail_count, head_count, head_width)
        .astype(jnp.bfloat16)
    )


def decode_keys(cache_rows, fresh_rows, slot_count):
    kv_count, head_width = (cache_rows.shape[2], cache_rows.shape[3])
    own_rows = cache_rows.reshape(
        slot_count, cache_rows.shape[0] // slot_count, 2, kv_count, head_width
    )
    new_rows = jnp.swapaxes(fresh_rows.reshape(2, slot_count, 2, kv_count, head_width), 0, 1)
    return (own_rows, new_rows)


def slot_state(query_rows, key_value, allowed):
    row_count, head_count, head_width = query_rows.shape
    slot_count, kv_count = (key_value.shape[0], key_value.shape[3])
    grouped = query_rows.reshape(2, slot_count, kv_count, head_count // kv_count, head_width)
    scores = jnp.einsum(
        "eskgd,sjkd->eskgj", grouped, key_value[:, :, 0], preferred_element_type=jnp.float32
    ) * (1.0 / math.sqrt(head_width))
    start_state = empty_state(scores.shape[:-1], head_width)
    return merge_block(
        start_state, scores, allowed[:, :, None, None, :], key_value[:, :, 1], "eskgj,sjkd->eskgd"
    )


def body(
    request_dest,
    request_slot,
    page_len,
    page_rows,
    kv_cache,
    decode_cache,
    prefix_len,
    cached_len,
    queries,
    fresh_kv,
):
    members = lax.axis_size("inst")
    request_count = request_dest.shape[1]
    slot_count = cached_len.shape[1]
    row_count, head_count, head_width = (queries.shape[1], queries.shape[2], queries.shape[3])
    tail_count = row_count - 2 * slot_count
    page_depth = page_rows.shape[2]
    page_shape = page_rows.shape[2:]
    step_queries = queries[0, tail_count:]
    targets = request_dest[0]
    req_order = jnp.arange(request_count, dtype=jnp.int32)
    earlier = (targets[:, None] == targets[None, :]) & (req_order[None, :] < req_order[:, None])
    placing = jnp.sum(earlier.astype(jnp.int32), axis=1)
    outgoing = (
        jnp.zeros((members, PAIR) + page_shape, page_rows.dtype)
        .at[targets, placing]
        .set(page_rows[0], mode="drop")
    )
    slot_out = (
        jnp.full((members, PAIR), -1, jnp.int32)
        .at[targets, placing]
        .set(request_slot[0], mode="drop")
    )
    length_out = (
        jnp.zeros((members, PAIR), jnp.int32).at[targets, placing].set(page_len[0], mode="drop")
    )
    own_rows, new_rows = decode_keys(decode_cache[0], fresh_kv[0, tail_count:], slot_count)
    arrived, slot_in, length_in = (
        lax.all_to_all(outgoing, "inst", split_axis=0, concat_axis=0, tiled=True),
        lax.all_to_all(slot_out, "inst", split_axis=0, concat_axis=0, tiled=True),
        lax.all_to_all(length_out, "inst", split_axis=0, concat_axis=0, tiled=True),
    )
    where_to = jnp.where(slot_in >= 0, slot_in, slot_count).reshape(-1)
    slot_pages = (
        jnp.zeros((slot_count,) + page_shape, page_rows.dtype)
        .at[where_to]
        .set(arrived.reshape((-1,) + page_shape), mode="drop")
    )
    slot_lengths = (
        jnp.zeros((slot_count,), jnp.int32).at[where_to].set(length_in.reshape(-1), mode="drop")
    )
    allowed = slot_mask(cached_len[0], slot_lengths, own_rows.shape[1], page_depth)
    key_value = jnp.concatenate([own_rows, slot_pages, new_rows], 1)
    local_max, local_sum, local_summed = slot_state(step_queries, key_value, allowed)
    mixed = local_summed / local_sum[..., None]
    step_out = mixed.reshape(2 * slot_count, head_count, head_width).astype(jnp.bfloat16)
    tail_out = tail_attention(
        queries[0, :tail_count], kv_cache[0], fresh_kv[0, :tail_count], prefix_len[0]
    )
    return jnp.concatenate([tail_out, step_out], 0)[None]


def solution(mesh):
    placed = (
        P(("groups", "inst"), None),
        P(("groups", "inst"), None),
        P(("groups", "inst"), None),
        P(("groups", "inst"), None, None, None, "tp", None),
        P(("groups", "inst"), None, None, "tp", None),
        P(("groups", "inst"), None, None, "tp", None),
        P(("groups", "inst")),
        P(("groups", "inst"), None),
        P(("groups", "inst"), None, "tp", None),
        P(("groups", "inst"), None, None, "tp", None),
    )
    return jax.shard_map(
        body,
        mesh=mesh,
        in_specs=placed,
        out_specs=P(("groups", "inst"), None, "tp", None),
        check_vma=False,
    )
```

profile of v0, /device:TPU:0, one launch (start us, length us, event | category | flops | bytes accessed | tf_op | source)
XLA Modules:
  0.0 128.6 jit_solution(8005276949234681534)
XLA Ops:
  0.0 1.0 convert_reduce_fusion
  1.0 0.7 fusion.46
  1.7 1.4 %scatter_fusion = s32[8,2]{0,1:T(2,128)S(1)} fusion(s32[8,2]{0,1:T(2,128)S(1)} %broadcast.179, s32[8]{0:T(128)S(1)} %fusion.46, s32[8]{0:T(128)} %bitcast.150), kind=kCustom, calls=%fused_computation | custom fusion | bytes 160 | tf_op jit(solution)/shard_map/scatter | solution.py:153
  3.1 0.7 copy.58
  3.8 7.3 %all-to-all-start = ((s32[8,1,2]{2,1,0:T(1,128)}), s32[8,1,2]{2,1,0:T(1,128)S(1)}, u32[]{:S(2)}, u32[]{:S(2)}) async-start(s32[8,1,2]{2,1,0:T(1,128)} %copy.58), calls=%async_computation | async-start | bytes 8192 | tf_op jit(solution)/shard_map/all_to_all | solution.py:161
  11.1 3.4 %slice.38 = bf16[1,256,32,128]{3,2,1,0:T(8,128)(2,1)} slice(bf16[1,272,32,128]{3,2,1,0:T(8,128)(2,1)} %param.20), slice={[0:1], [0:256], [0:32], [0:128]} | slice | bytes 4194304 | tf_op jit(solution)/shard_map/slice | solution.py:179
  14.6 0.1 copy.61
  14.7 1.6 %copy.91 = bf16[1,1024,2,4,128]{4,1,3,2,0:T(8,128)(2,1)} copy(bf16[1,1024,2,4,128]{4,3,2,1,0:T(4,128)(2,1)S(1)} %copy-done.2) | data formatting | bytes 4194304 | tf_op args[4]
  16.3 0.7 copy-done.1
  17.1 0.8 copy.55
  17.9 56.8 %while.18 = (s32[]{:T(128)}, f32[4,8,256]{2,1,0:T(8,128)S(1)}, f32[4,8,256]{2,1,0:T(8,128)S(1)}, f32[4,8,256,128]{3,2,1,0:T(8,128)}, s32[]{:T(128)}, /*index=5*/...) while((s32[]{:T(128)}, f32[4,8,256]{2,1,0:T(8,128)S(1)}, ...), condition=%wide.region_3.0_spmd.clone, body=%wide.region_0.3_spmd.clone.sunk | while | flops 2205197312 | bytes 62393044 | solution.py:76
  17.9 0.7 add_compare_fusion.2
  18.7 8.1 %bitcast_reduce_fusion.2 = (f32[4,8,256]{2,1,0:T(8,128)S(1)}, f32[4,512,256,8]{2,1,3,0:T(8,128)}) fusion(pred[512]{0:T(512)(128)(4,1)S(1)} %add_compare_fusion.2, bf16[256,4,8,128]{3,0,2,1:T(8,128)(2,1)S(1)} %get-tuple-element.265, bf16[1024,2,4,128]{3,0,2,1:T(8,128)(2,1)} %get-tuple-element.264, s32[]{:T(128)S(6)} %select_n.174), kind=kOutput, calls=%fused_computation.6.clone.1 | convolution fusion | flops 1086316544 | bytes 19431940 | tf_op jit(solution)/shard_map/while/body/eval_jaxpr/tkgd,jkd->kgtj/dot_general | solution.py:65
  26.8 8.2 %fusion.65 = f32[4,8,256]{2,1,0:T(8,128)S(1)} fusion(f32[4,512,256,8]{2,1,3,0:T(8,128)} %get-tuple-element.232, f32[4,8,256]{2,1,0:T(8,128)S(1)} %select_maximum_fusion.2, pred[512]{0:T(512)(128)(4,1)S(1)} %add_compare_fusion.2), kind=kLoop, calls=%fused_computation.11.clone.1 | loop fusion | flops 20963328 | bytes 16843264 | tf_op jit(solution)/shard_map/while/body/eval_jaxpr/reduce_sum | solution.py:20
  35.0 11.0 %fusion.67 = f32[4,8,256,128]{3,2,1,0:T(8,128)} fusion(f32[4,8,256,128]{3,2,1,0:T(8,128)} %get-tuple-element.250, f32[4,8,256]{2,1,0:T(8,128)S(1)} %get-tuple-element.234, pred[]{:T(512)S(6)} %compare.21, f32[4,512,256,8]{2,1,3,0:T(8,128)} %get-tuple-element.232, f32[4,8,256]{2,1,0:T(8,128)S(1)} %select_maximum_fusion.2, ...), kind=kOutput, calls=%fused_computation.16.clone.1 | convolution fusion | flops 1097859072 | bytes 25756680 | tf_op jit(solution)/shard_map/while/body/eval_jaxpr/kgtj,jkd->kgtd/dot_general | solution.py:21
  46.0 0.7 add_compare_fusion.2
  46.7 8.1 %bitcast_reduce_fusion.2 = (f32[4,8,256]{2,1,0:T(8,128)S(1)}, f32[4,512,256,8]{2,1,3,0:T(8,128)}) fusion(pred[512]{0:T(512)(128)(4,1)S(1)} %add_compare_fusion.2, bf16[256,4,8,128]{3,0,2,1:T(8,128)(2,1)S(1)} %get-tuple-element.265, bf16[1024,2,4,128]{3,0,2,1:T(8,128)(2,1)} %get-tuple-element.264, s32[]{:T(128)S(6)} %select_n.174), kind=kOutput, calls=%fused_computation.6.clone.1 | convolution fusion | flops 1086316544 | bytes 19431940 | tf_op jit(solution)/shard_map/while/body/eval_jaxpr/tkgd,jkd->kgtj/dot_general | solution.py:65
  54.8 8.2 %fusion.65 = f32[4,8,256]{2,1,0:T(8,128)S(1)} fusion(f32[4,512,256,8]{2,1,3,0:T(8,128)} %get-tuple-element.232, f32[4,8,256]{2,1,0:T(8,128)S(1)} %select_maximum_fusion.2, pred[512]{0:T(512)(128)(4,1)S(1)} %add_compare_fusion.2), kind=kLoop, calls=%fused_computation.11.clone.1 | loop fusion | flops 20963328 | bytes 16843264 | tf_op jit(solution)/shard_map/while/body/eval_jaxpr/reduce_sum | solution.py:20
  63.0 11.7 %fusion.67 = f32[4,8,256,128]{3,2,1,0:T(8,128)} fusion(f32[4,8,256,128]{3,2,1,0:T(8,128)} %get-tuple-element.250, f32[4,8,256]{2,1,0:T(8,128)S(1)} %get-tuple-element.234, pred[]{:T(512)S(6)} %compare.21, f32[4,512,256,8]{2,1,3,0:T(8,128)} %get-tuple-element.232, f32[4,8,256]{2,1,0:T(8,128)S(1)} %select_maximum_fusion.2, ...), kind=kOutput, calls=%fused_computation.16.clone.1 | convolution fusion | flops 1097859072 | bytes 25756680 | tf_op jit(solution)/shard_map/while/body/eval_jaxpr/kgtj,jkd->kgtd/dot_general | solution.py:21
  74.7 0.9 copy.92
  75.6 0.8 scatter_fusion.1
  76.4 2.3 %fusion.18 = (f32[4,8,256]{2,1,0:T(8,128)S(1)}, f32[4,256,256,8]{2,1,3,0:T(8,128)S(1)}) fusion(pred[256,256]{0,1:T(8,128)(4,1)S(1)} %iota_compare_fusion, bf16[256,4,8,128]{3,0,2,1:T(8,128)(2,1)S(1)} %get-tuple-element.271, bf16[256,2,4,128]{3,0,2,1:T(8,128)(2,1)} %bitcast.143), kind=kOutput, calls=%fused_computation.32 | convolution fusion | flops 543154176 | bytes 10846208 | tf_op jit(solution)/shard_map/tkgd,jkd->kgtj/dot_general | solution.py:83
  78.7 2.1 %fusion.19 = f32[4,8,256]{2,1,0:T(8,128)S(1)} fusion(f32[4,256,256,8]{2,1,3,0:T(8,128)S(1)} %get-tuple-element.183, f32[4,8,256]{2,1,0:T(8,128)S(1)} %max.10, pred[256,256]{0,1:T(8,128)(4,1)S(1)} %iota_compare_fusion), kind=kLoop, calls=%fused_computation.33 | loop fusion | flops 10477568 | bytes 8519680 | tf_op jit(solution)/shard_map/reduce_sum | solution.py:20
  80.8 1.1 copy-done
  81.9 0.7 copy.59
  82.6 6.0 %all-to-all-start.1 = ((s32[8,1,2]{2,1,0:T(1,128)}), s32[8,1,2]{2,1,0:T(1,128)S(1)}, u32[]{:S(2)}, u32[]{:S(2)}) async-start(s32[8,1,2]{2,1,0:T(1,128)} %copy.59), calls=%async_computation.1 | async-start | bytes 8192 | tf_op jit(solution)/shard_map/all_to_all | solution.py:162
  88.6 1.2 broadcast_in_dim.167
  89.8 2.5 %scatter_fusion.2 = bf16[8,2,32,2,4,128]{5,2,4,3,1,0:T(8,128)(2,1)} fusion(bf16[8,2,32,2,4,128]{5,2,4,3,1,0:T(8,128)(2,1)} %broadcast_in_dim.167, s32[8]{0:T(128)S(1)} %fusion.46, bf16[8,32,2,4,128]{4,1,3,2,0:T(8,128)(2,1)S(1)} %copy.61), kind=kCustom, calls=%fused_computation.3 | custom fusion | bytes 1572928 | tf_op jit(solution)/shard_map/scatter | solution.py:148
  92.3 2.8 %all-to-all-done.1 = s32[8,1,2]{2,1,0:T(1,128)S(1)} async-done(((s32[8,1,2]{2,1,0:T(1,128)}), s32[8,1,2]{2,1,0:T(1,128)S(1)}, u32[]{:S(2)}, u32[]{:S(2)}) %all-to-all-start.1) | async-done | bytes 96 | tf_op jit(solution)/shard_map/all_to_all | solution.py:162
  95.1 4.4 %all-to-all-start.2 = ((bf16[8,2,32,2,4,128]{5,2,4,3,1,0:T(8,128)(2,1)}), bf16[8,2,32,2,4,128]{5,2,4,3,1,0:T(8,128)(2,1)}, u32[]{:S(2)}, u32[]{:S(2)}) async-start(bf16[8,2,32,2,4,128]{5,2,4,3,1,0:T(8,128)(2,1)} %scatter_fusion.2), calls=%async_computation.2 | async-start | bytes 2097152 | tf_op jit(solution)/shard_map/all_to_all | solution.py:160
  99.5 7.4 %divide_convert_fusion = bf16[4,8,256,128]{3,2,1,0:T(8,128)(2,1)S(1)} fusion(f32[4,8,256,128]{3,2,1,0:T(8,128)} %get-tuple-element.131, f32[4,8,256]{2,1,0:T(8,128)S(1)} %get-tuple-element.174, f32[4,8,256]{2,1,0:T(8,128)S(1)} %get-tuple-element.175, f32[4,256,256,8]{2,1,3,0:T(8,128)} %copy-done, f32[4,8,256]{2,1,0:T(8,128)S(1)} %max.10, ...), kind=kOutput, calls=%fused_computation.36 | convolution fusion | flops 551550976 | bytes 15106048 | tf_op jit(solution)/shard_map/kgtj,jkd->kgtd/dot_general | solution.py:21
  106.9 1.4 %copy.68 = bf16[256,32,128]{2,1,0:T(8,128)(2,1)S(1)} copy(bf16[256,32,128]{2,0,1:T(8,128)(2,1)S(1)} %bitcast.142) | data formatting | bytes 4194304 | tf_op jit(solution)/shard_map/convert_element_type | solution.py:95
  108.3 0.1 iota_compare_fusion.3
  108.4 0.6 broadcast.276
  109.0 0.7 reduce.6
  109.7 0.1 all_to_all.19
  109.8 0.7 reduce.7
  110.5 0.1 reshape.202
  110.6 0.6 scatter_custom_fusion.2
  111.3 0.1 pad_add_fusion
  111.4 12.0 %all-to-all-done.2 = bf16[8,2,32,2,4,128]{5,2,4,3,1,0:T(8,128)(2,1)} async-done(((bf16[8,2,32,2,4,128]{5,2,4,3,1,0:T(8,128)(2,1)}), bf16[8,2,32,2,4,128]{5,2,4,3,1,0:T(8,128)(2,1)}, u32[]{:S(2)}, u32[]{:S(2)}) %all-to-all-start.2) | async-done | bytes 1048608 | tf_op jit(solution)/shard_map/all_to_all | solution.py:160
  123.4 0.1 broadcast_in_dim.166
  123.5 2.3 %scatter_fusion.3 = bf16[8,32,2,4,128]{4,1,3,2,0:T(8,128)(2,1)S(1)} fusion(bf16[8,32,2,4,128]{4,1,3,2,0:T(8,128)(2,1)S(1)} %broadcast_in_dim.166, s32[16]{0:T(128)S(1)} %fusion.45, bf16[16,32,2,4,128]{4,1,3,2,0:T(8,128)(2,1)} %bitcast.25), kind=kCustom, calls=%fused_computation.4 | custom fusion | bytes 3145792 | tf_op jit(solution)/shard_map/scatter | solution.py:168
  125.8 0.1 pad_maximum_fusion
  125.9 0.4 fusion.54
  126.3 0.3 fusion.36
  126.7 0.3 fusion.32
  127.0 1.6 %maximum_bitcast_fusion = bf16[1,272,32,128]{3,2,1,0:T(8,128)(2,1)} fusion(bf16[16,32,128]{2,1,0:T(8,128)(2,1)S(1)} %bitcast.145, bf16[256,32,128]{2,1,0:T(8,128)(2,1)S(1)} %copy.68), kind=kLoop, calls=%fused_computation.42 | loop fusion | flops 1114112 | bytes 4456448 | tf_op jit(solution)/shard_map/broadcast_in_dim | solution.py:181
  (47 shorter events, 0.4 us)
Async XLA Ops:
  0.0 14.5 %slice-start.1 = ((bf16[1,272,2,4,128]{4,3,2,1,0:T(4,128)(2,1)}), bf16[1,16,2,4,128]{4,3,2,1,0:T(4,128)(2,1)S(1)}, s32[]{:S(2)}) async-start(bf16[1,272,2,4,128]{4,3,2,1,0:T(4,128)(2,1)} %param.21), calls=%async_computation.4 | async-start | bytes 65536 | tf_op jit(solution)/shard_map/slice | solution.py:158
  0.0 14.6 %copy-start.5 = (bf16[1,64,2,4,128]{4,3,2,1,0:T(4,128)(2,1)S(1)}, bf16[1,64,2,4,128]{4,3,2,1,0:T(4,128)(2,1)}, u32[]{:S(2)}) copy-start(bf16[1,64,2,4,128]{4,3,2,1,0:T(4,128)(2,1)} %param.17) | copy-start | bytes 393220
  0.0 14.7 %copy-start.2 = (bf16[1,1024,2,4,128]{4,3,2,1,0:T(4,128)(2,1)S(1)}, bf16[1,1024,2,4,128]{4,3,2,1,0:T(4,128)(2,1)}, u32[]{:S(2)}) copy-start(bf16[1,1024,2,4,128]{4,3,2,1,0:T(4,128)(2,1)} %param.16) | copy-start | bytes 6291460
  3.8 78.8 %all-to-all-start = ((s32[8,1,2]{2,1,0:T(1,128)}), s32[8,1,2]{2,1,0:T(1,128)S(1)}, u32[]{:S(2)}, u32[]{:S(2)}) async-start(s32[8,1,2]{2,1,0:T(1,128)} %copy.58), calls=%async_computation | async-start | bytes 8192 | tf_op jit(solution)/shard_map/all_to_all | solution.py:161
  11.1 3.5 %copy-start.4 = (bf16[1,8,32,2,4,128]{5,4,3,2,1,0:T(4,128)(2,1)S(1)}, bf16[1,8,32,2,4,128]{5,4,3,2,1,0:T(4,128)(2,1)}, u32[]{:S(2)}) copy-start(bf16[1,8,32,2,4,128]{5,4,3,2,1,0:T(4,128)(2,1)} %param.15) | copy-start | bytes 1572868
  14.7 2.3 %copy-start.1 = (bf16[1,256,32,128]{3,2,1,0:T(8,128)(2,1)S(1)}, bf16[1,256,32,128]{3,2,1,0:T(8,128)(2,1)}, u32[]{:S(2)}) copy-start(bf16[1,256,32,128]{3,2,1,0:T(8,128)(2,1)} %slice.38) | copy-start | bytes 6291460
  17.9 56.8 %slice-start.2 = ((bf16[1,272,2,4,128]{4,3,2,1,0:T(4,128)(2,1)}), bf16[1,256,2,4,128]{4,3,2,1,0:T(4,128)(2,1)S(1)}, s32[]{:S(2)}) async-start(bf16[1,272,2,4,128]{4,3,2,1,0:T(4,128)(2,1)} %param.21), calls=%async_computation.5 | async-start | bytes 1048576 | tf_op jit(solution)/shard_map/slice | solution.py:179
  17.9 57.6 %copy-start.6 = (s32[1,8]{1,0:T(1,128)S(1)}, s32[1,8]{1,0:T(1,128)}, u32[]{:S(2)}) copy-start(s32[1,8]{1,0:T(1,128)} %param.14) | copy-start | bytes 100
  78.7 3.2 %copy-start = (f32[4,256,256,8]{2,1,3,0:T(8,128)}, f32[4,256,256,8]{2,1,3,0:T(8,128)S(1)}, u32[]{:S(2)}) copy-start(f32[4,256,256,8]{2,1,3,0:T(8,128)S(1)} %get-tuple-element.183) | copy-start | bytes 25165828
  81.9 17.6 %copy-start.3 = (bf16[1,256,2,4,128]{4,1,3,2,0:T(8,128)(2,1)S(1)}, bf16[1,256,2,4,128]{4,1,3,2,0:T(8,128)(2,1)}, u32[]{:S(2)}) copy-start(bf16[1,256,2,4,128]{4,1,3,2,0:T(8,128)(2,1)} %copy.92) | copy-start | bytes 1572868
  82.6 12.4 %all-to-all-start.1 = ((s32[8,1,2]{2,1,0:T(1,128)}), s32[8,1,2]{2,1,0:T(1,128)S(1)}, u32[]{:S(2)}, u32[]{:S(2)}) async-start(s32[8,1,2]{2,1,0:T(1,128)} %copy.59), calls=%async_computation.1 | async-start | bytes 8192 | tf_op jit(solution)/shard_map/all_to_all | solution.py:162
  95.1 28.3 %all-to-all-start.2 = ((bf16[8,2,32,2,4,128]{5,2,4,3,1,0:T(8,128)(2,1)}), bf16[8,2,32,2,4,128]{5,2,4,3,1,0:T(8,128)(2,1)}, u32[]{:S(2)}, u32[]{:S(2)}) async-start(bf16[8,2,32,2,4,128]{5,2,4,3,1,0:T(8,128)(2,1)} %scatter_fusion.2), calls=%async_computation.2 | async-start | bytes 2097152 | tf_op jit(solution)/shard_map/all_to_all | solution.py:160
  106.9 1.4 %copy-start.7 = (s32[1,8]{1,0:T(1,128)S(1)}, s32[1,8]{1,0:T(1,128)}, u32[]{:S(2)}) copy-start(s32[1,8]{1,0:T(1,128)} %param.19) | copy-start | bytes 100
  106.9 19.0 %slice-start = ((bf16[1,272,32,128]{3,2,1,0:T(8,128)(2,1)}), bf16[1,16,32,128]{3,2,1,0:T(8,128)(2,1)S(1)}, s32[]{:S(2)}) async-start(bf16[1,272,32,128]{3,2,1,0:T(8,128)(2,1)} %param.20), calls=%async_computation.3 | async-start | bytes 262144 | tf_op jit(solution)/shard_map/slice | solution.py:140
where the time goes:
time: 129 us
  matrix products  49.2 us (38%)
  other arithmetic  25.3 us (20%)
  local copies, waits for them, and re-layouts  21.1 us (16%)
  starting transfers between devices  17.7 us (14%)
  waiting for transfers between devices  14.8 us (11%)
    dot_general x4, matrix products, merge_block(): jnp.einsum(einsum_form, weights.astype(jnp.bfloat16), values, preferred_e...  30.4 us
    reduce_sum x4, other arithmetic, merge_block(): weight_sum = weight_sum * shrink + jnp.sum(weights, axis=-1)  18.8 us
    dot_general x2, matrix products, visit_block(): jnp.einsum('tkgd,jkd->kgtj', grouped, block_kv[:, 0], preferred_element_t...  16.2 us
    all_to_all x1, waiting for transfers between devices, body(): lax.all_to_all(outgoing, 'inst', split_axis=0, concat_axis=0, tiled=True)  12 us
    all_to_all x1, starting transfers between devices, body(): lax.all_to_all(slot_out, 'inst', split_axis=0, concat_axis=0, tiled=True)  7.29 us
    all_to_all x1, starting transfers between devices, body(): lax.all_to_all(length_out, 'inst', split_axis=0, concat_axis=0, tiled=True)  5.98 us
    all_to_all x1, starting transfers between devices, body(): lax.all_to_all(outgoing, 'inst', split_axis=0, concat_axis=0, tiled=True)  4.43 us
    unnamed x19, local copies, waits for them, and re-layouts  4.32 us
  transfers between devices with their start and end apart: 3, of which 2 were waited for; matrix products, arithmetic and copies ran while one was open for 66% of the time, Pallas kernels for 0%

commit v1 on v0

v1 whole, which is shorter than its diff:
```python
import functools
import math

import jax
import jax.numpy as jnp
from jax import lax
from jax.experimental import pallas as pl
from jax.experimental.pallas import tpu as pltpu
from jax.sharding import PartitionSpec as P

PAIR = 2
NEG = -1e30
F32 = jnp.float32
BF16 = jnp.bfloat16
META = 16
MIB = 1 << 20


def nt_dot(a, b):
    return lax.dot_general(a, b, (((1,), (1,)), ((), ())), preferred_element_type=F32)


def nn_dot(a, b):
    return jnp.dot(a, b, preferred_element_type=F32)


def unmix(kinds, rows):
    keys = rows // kinds
    i = lax.broadcasted_iota(jnp.int32, (rows, rows), 0)
    j = lax.broadcasted_iota(jnp.int32, (rows, rows), 1)
    return jnp.where(j == (i % keys) * kinds + i // keys, 1.0, 0.0).astype(BF16)


def scaled_queries(q, scale):
    q = q * scale
    high = q.astype(BF16)
    low = (q - high.astype(F32)).astype(BF16)
    return jnp.concatenate([high, low], axis=1)


def twice(k):
    return jnp.concatenate([k, k], axis=1)


def with_ones(v):
    return jnp.concatenate([v, jnp.ones_like(v)], axis=1)


def pack_kernel(split, me_ref, dest_ref, slot_ref, len_ref, pages_ref, *refs):
    if split:
        members = len(refs) - 5
        buffers = refs[:members]
    else:
        members = refs[0].shape[0]
        buffers = [refs[0].at[k] for k in range(members)]
    zeros, meta, page_sem, meta_sem, zero_sem = refs[-5:]
    requests = pages_ref.shape[0]
    page_rows = pages_ref.shape[1]
    depth = 32
    me = me_ref[0]
    peer, place = [], []
    for r in range(requests):
        target = dest_ref[0, r]
        earlier = jnp.int32(0)
        for q in range(r):
            earlier = earlier + jnp.where(dest_ref[0, q] == target, 1, 0)
        peer.append(target ^ me if split else target)
        place.append(earlier)
    for r in range(requests):
        begin = pl.multiple_of(place[r] * page_rows, page_rows)
        if split:
            for k in range(members):

                @pl.when(peer[r] == k)
                def _():
                    pltpu.make_async_copy(
                        pages_ref.at[r], buffers[k].at[pl.ds(begin, page_rows), :], page_sem
                    ).start()

        else:
            pltpu.make_async_copy(
                pages_ref.at[r], refs[0].at[peer[r], pl.ds(begin, page_rows), :], page_sem
            ).start()
    zeros[...] = jnp.zeros_like(zeros)
    lane = lax.broadcasted_iota(jnp.int32, (META, 128), 1)
    half = (lane // depth) % PAIR
    used = []
    for k in range(members):
        code = jnp.full((META, 128), -1.0, F32)
        count = jnp.int32(0)
        for r in range(requests):
            mine = peer[r] == k
            count = count + jnp.where(mine, 1, 0)
            live = jnp.where(mine, len_ref[0, r], 0)
            here = (half == place[r]) & (lane % depth < live)
            code = jnp.where(here, slot_ref[0, r].astype(F32), code)
        meta[k] = code.astype(BF16)
        used.append(count)
        pltpu.make_async_copy(
            meta.at[k], buffers[k].at[pl.ds(PAIR * page_rows, META), :], meta_sem
        ).start()

        @pl.when(count == 0)
        def _():
            pltpu.make_async_copy(
                zeros, buffers[k].at[pl.ds(0, PAIR * page_rows), :], zero_sem
            ).start()

    for r in range(requests):
        pltpu.make_async_copy(
            pages_ref.at[0], buffers[0].at[pl.ds(0, page_rows), :], page_sem
        ).wait()
    for k in range(members):
        pltpu.make_async_copy(
            meta.at[k], buffers[k].at[pl.ds(PAIR * page_rows, META), :], meta_sem
        ).wait()

        @pl.when(used[k] == 0)
        def _():
            pltpu.make_async_copy(
                zeros, buffers[k].at[pl.ds(0, PAIR * page_rows), :], zero_sem
            ).wait()


def pack(split, members, me, dest, slot, length, pages):
    rows = PAIR * pages.shape[1] + META
    if split:
        out_shape = [jax.ShapeDtypeStruct((rows, 128), BF16)] * members
    else:
        out_shape = [jax.ShapeDtypeStruct((members, rows, 128), BF16)]
    smem = pl.BlockSpec(memory_space=pltpu.SMEM)
    hbm = pl.BlockSpec(memory_space=pl.ANY)
    return pl.pallas_call(
        functools.partial(pack_kernel, split),
        out_shape=out_shape,
        in_specs=[smem] * 4 + [hbm],
        out_specs=[hbm] * len(out_shape),
        scratch_shapes=[
            pltpu.VMEM((PAIR * pages.shape[1], 128), BF16),
            pltpu.VMEM((members, META, 128), BF16),
            pltpu.SemaphoreType.DMA,
            pltpu.SemaphoreType.DMA,
            pltpu.SemaphoreType.DMA,
        ],
        name="pack_pages",
    )(me, dest, slot, length, pages)


def tail_kernel(scale, prefix_ref, q_ref, cache_ref, fresh_ref, o_ref, keys, values, mixed):
    block, heads, width = q_ref.shape[1:]
    kv_heads = keys.shape[0]
    group = heads // kv_heads
    kinds = 2 * kv_heads
    context = cache_ref.shape[0] // kinds
    total = keys.shape[1]
    step = pl.program_id(0)

    @pl.when(step == 0)
    def _():
        order = unmix(kinds, 256)
        depth = 256 // kinds
        for at in range(0, total, 2 * depth):
            source, base = (cache_ref, at) if at < context else (fresh_ref, at - context)
            first = source[base * kinds : base * kinds + 256, :]
            second = source[base * kinds + 256 : base * kinds + 512, :]
            sorted_rows = nn_dot(order, jnp.concatenate([first, second], axis=1)).astype(BF16)
            for half in range(2):
                spot = slice(at + half * depth, at + (half + 1) * depth)
                for h in range(kv_heads):
                    rows = sorted_rows[:, half * width : (half + 1) * width]
                    keys[h, spot, :] = rows[h * depth : (h + 1) * depth]
                    values[h, spot, :] = rows[(kv_heads + h) * depth : (kv_heads + h + 1) * depth]

    rows = block * group
    prefix = prefix_ref[0]
    column = lax.broadcasted_iota(jnp.int32, (rows, total), 1)
    row = step * block + lax.broadcasted_iota(jnp.int32, (rows, total), 0) // group
    limit = jnp.where(column < context, prefix, row + context + 1)
    allowed = column < limit
    queries = q_ref[0].astype(F32).reshape(block, kv_heads, group, width)
    for h in range(kv_heads):
        q = scaled_queries(queries[:, h].reshape(rows, width), scale)
        scores = jnp.where(allowed, nt_dot(q, twice(keys[h])), NEG)
        peak = jnp.max(scores, axis=1, keepdims=True)
        weights = jnp.exp2(scores - peak).astype(BF16)
        summed = nn_dot(weights, with_ones(values[h]))
        out = summed[:, :width] / summed[:, width:]
        mixed[:, h] = out.reshape(block, group, width)
    o_ref[0] = mixed[...].reshape(block, heads, width).astype(BF16)


def tail_attention(prefix, queries, cache, fresh, tail_count, kv_heads):
    _, row_count, heads, width = queries.shape
    block = 32
    context = cache.shape[0] // (2 * kv_heads)
    total = context + tail_count
    scale = math.log2(math.e) / math.sqrt(width)
    spec = pl.BlockSpec((1, block, heads, width), lambda i: (0, i, 0, 0))
    whole = lambda a: pl.BlockSpec(a.shape, lambda i: (0, 0))
    return pl.pallas_call(
        functools.partial(tail_kernel, scale),
        grid=(tail_count // block,),
        out_shape=jax.ShapeDtypeStruct(queries.shape, BF16),
        in_specs=[pl.BlockSpec(memory_space=pltpu.SMEM), spec, whole(cache), whole(fresh)],
        out_specs=spec,
        scratch_shapes=[
            pltpu.VMEM((kv_heads, total, width), BF16),
            pltpu.VMEM((kv_heads, total, width), BF16),
            pltpu.VMEM((block, kv_heads, heads // kv_heads, width), F32),
        ],
        compiler_params=pltpu.CompilerParams(vmem_limit_bytes=40 * MIB),
        cost_estimate=pl.CostEstimate(
            flops=4 * tail_count * heads * total * width * 4,
            bytes_accessed=8 * MIB,
            transcendentals=tail_count * heads * total,
        ),
        name="tail_attention",
    )(prefix, queries, cache, fresh)


def row_place(rows, columns, group, slots):
    row = lax.broadcasted_iota(jnp.int32, (rows, columns), 0) // group
    return row % slots, row // slots


def local_kernel(scale, slots, code_ref, q_ref, own_ref, new_ref, m_ref, l_ref, a_ref, keys, values):
    count, heads, width = q_ref.shape
    kv_heads = keys.shape[0]
    group = heads // kv_heads
    kinds = 2 * kv_heads
    for source, base in ((own_ref, 0), (new_ref, own_ref.shape[0] // kinds)):
        chunk = min(256, source.shape[0])
        order = unmix(kinds, chunk)
        depth = chunk // kinds
        for at in range(source.shape[0] // chunk):
            sorted_rows = nn_dot(order, source[at * chunk : (at + 1) * chunk, :]).astype(BF16)
            spot = slice(base + at * depth, base + (at + 1) * depth)
            for h in range(kv_heads):
                keys[h, spot, :] = sorted_rows[h * depth : (h + 1) * depth]
                values[h, spot, :] = sorted_rows[(kv_heads + h) * depth : (kv_heads + h + 1) * depth]
    rows, total = count * group, keys.shape[1]
    slot, made = row_place(rows, total, group, slots)
    code = code_ref[...]
    allowed = (code == slot) | ((code >= slots) & (code - slots == slot)) | (
        (made >= 1) & (code - 2 * slots == slot)
    )
    queries = q_ref[...].astype(F32).reshape(count, kv_heads, group, width)
    for h in range(kv_heads):
        q = scaled_queries(queries[:, h].reshape(rows, width), scale)
        scores = jnp.where(allowed, nt_dot(q, twice(keys[h])), NEG)
        peak = jnp.max(scores, axis=1, keepdims=True)
        weights = jnp.exp2(scores - peak).astype(BF16)
        summed = nn_dot(weights, with_ones(values[h]))
        m_ref[h] = jnp.broadcast_to(peak, (rows, width))
        l_ref[h] = summed[:, width:]
        a_ref[h] = summed[:, :width]


def local_state(codes, queries, own, new, slots, kv_heads):
    count, heads, width = queries.shape
    rows = count * heads // kv_heads
    total = (own.shape[0] + new.shape[0]) // (2 * kv_heads)
    scale = math.log2(math.e) / math.sqrt(width)
    state = jax.ShapeDtypeStruct((kv_heads, rows, width), F32)
    return pl.pallas_call(
        functools.partial(local_kernel, scale, slots),
        out_shape=[state] * 3,
        scratch_shapes=[
            pltpu.VMEM((kv_heads, total, width), BF16),
            pltpu.VMEM((kv_heads, total, width), BF16),
        ],
        compiler_params=pltpu.CompilerParams(vmem_limit_bytes=40 * MIB),
        cost_estimate=pl.CostEstimate(
            flops=8 * rows * kv_heads * total * width,
            bytes_accessed=3 * MIB,
            transcendentals=rows * kv_heads * total,
        ),
        name="decode_local",
    )(codes, queries, own, new)


def page_kernel(scale, slots, split, q_ref, m_ref, l_ref, a_ref, out_in, *refs):
    out_ref, keys, values, mixed, staged, sem = refs[-6:]
    arrived = refs[:-6]
    count, heads, width = q_ref.shape
    kv_heads = keys.shape[0]
    group = heads // kv_heads
    kinds = 2 * kv_heads
    order = unmix(kinds, 256)
    depth = 256 // kinds
    if split:
        piece = lambda k, a, b: arrived[k][a:b, :]
        members = len(arrived)
    else:
        piece = lambda k, a, b: arrived[0][k, a:b, :]
        members = arrived[0].shape[0]
    rows = count * group
    per = 8
    queries = q_ref[...].astype(F32).reshape(count, kv_heads, group, width)
    scaled = [scaled_queries(queries[:, h].reshape(rows, width), scale) for h in range(kv_heads)]
    state = [(m_ref[h], l_ref[h], a_ref[h]) for h in range(kv_heads)]
    lane = lax.broadcasted_iota(jnp.int32, (1, 128), 1)
    for begin in range(0, members, per):
        codes = []
        for k in range(per):
            both = jnp.concatenate(
                [piece(begin + k, 0, 256), piece(begin + k, 256, 512)], axis=1
            )
            sorted_rows = nn_dot(order, both).astype(BF16)
            for half in range(PAIR):
                at = (PAIR * k + half) * depth
                part = sorted_rows[:, half * width : (half + 1) * width]
                for h in range(kv_heads):
                    keys[h, at : at + depth, :] = part[h * depth : (h + 1) * depth]
                    values[h, at : at + depth, :] = part[
                        (kv_heads + h) * depth : (kv_heads + h + 1) * depth
                    ]
            codes.append(piece(begin + k, 512, 512 + META).astype(F32)[0:1, :])
        code = jnp.concatenate(
            [jnp.where(lane < 64, codes[k], codes[k + 1]) for k in range(0, per, 2)], axis=1
        )
        slot, _ = row_place(rows, code.shape[1], group, slots)
        allowed = code == slot.astype(F32)
        for h in range(kv_heads):
            old_peak, old_sum, old = state[h]
            scores = jnp.where(allowed, nt_dot(scaled[h], twice(keys[h])), NEG)
            peak = jnp.maximum(old_peak, jnp.max(scores, axis=1, keepdims=True))
            weights = jnp.exp2(scores - peak[:, 0:1]).astype(BF16)
            summed = nn_dot(weights, with_ones(values[h]))
            shrink = jnp.exp2(old_peak - peak)
            state[h] = (
                peak,
                old_sum * shrink + summed[:, width:],
                old * shrink + summed[:, :width],
            )
    for h in range(kv_heads):
        _, weight_sum, summed = state[h]
        mixed[:, h] = (summed / weight_sum).reshape(count, group, width)
    staged[...] = mixed[...].reshape(count, heads, width).astype(BF16)
    tail_count = out_ref.shape[1] - count
    copy = pltpu.make_async_copy(staged, out_ref.at[0, pl.ds(tail_count, count)], sem)
    copy.start()
    copy.wait()


def page_attention(queries, state, out, arrived, slots, kv_heads, split):
    count, heads, width = queries.shape
    group = heads // kv_heads
    scale = math.log2(math.e) / math.sqrt(width)
    vmem = pl.BlockSpec(memory_space=pltpu.VMEM)
    hbm = pl.BlockSpec(memory_space=pl.ANY)
    return pl.pallas_call(
        functools.partial(page_kernel, scale, slots, split),
        out_shape=jax.ShapeDtypeStruct(out.shape, BF16),
        in_specs=[vmem] * 4 + [hbm] + [vmem] * len(arrived),
        out_specs=hbm,
        input_output_aliases={4: 0},
        scratch_shapes=[
            pltpu.VMEM((kv_heads, 8 * 64, width), BF16),
            pltpu.VMEM((kv_heads, 8 * 64, width), BF16),
            pltpu.VMEM((count, kv_heads, group, width), F32),
            pltpu.VMEM((count, heads, width), BF16),
            pltpu.SemaphoreType.DMA,
        ],
        compiler_params=pltpu.CompilerParams(vmem_limit_bytes=48 * MIB),
        name="decode_pages",
    )(queries, *state, out, *arrived)


def body(
    request_dest,
    request_slot,
    page_len,
    page_rows,
    kv_cache,
    decode_cache,
    prefix_len,
    cached_len,
    queries,
    fresh_kv,
):
    members = lax.axis_size("inst")
    slots = cached_len.shape[1]
    row_count, heads, width = queries.shape[1:]
    kv_heads = kv_cache.shape[3]
    tail_count = row_count - 2 * slots
    requests, page_depth = page_rows.shape[1:3]
    split = members <= 8
    me = lax.axis_index("inst").astype(jnp.int32)

    pages = page_rows.reshape(requests, page_depth * 2 * kv_heads, width)
    packed = pack(split, members, me.reshape(1), request_dest, request_slot, page_len, pages)
    if split:
        arrived = list(packed)
        for k in range(members - 1, 0, -1):
            arrived[k] = lax.ppermute(packed[k], "inst", [(i, i ^ k) for i in range(members)])
    else:
        arrived = [lax.all_to_all(packed[0], "inst", split_axis=0, concat_axis=0, tiled=True)]

    cache = kv_cache.reshape(-1, width)
    fresh = fresh_kv.reshape(-1, width)
    out = tail_attention(prefix_len, queries, cache, fresh, tail_count, kv_heads)

    step_queries = queries[0, tail_count:]
    own = decode_cache.reshape(-1, width)
    new = fresh[tail_count * 2 * kv_heads :]
    cache_depth = decode_cache.shape[1] // slots
    slot_ids = jnp.arange(slots, dtype=jnp.int32)
    alive = jnp.arange(cache_depth, dtype=jnp.int32)[None, :] < cached_len[0][:, None]
    own_code = jnp.where(alive, slot_ids[:, None], -4 * slots).reshape(-1)
    codes = jnp.concatenate([own_code, slot_ids + slots, slot_ids + 2 * slots])[None, :]
    state = local_state(codes, step_queries, own, new, slots, kv_heads)

    return page_attention(step_queries, state, out, arrived, slots, kv_heads, split)


def solution(mesh):
    placed = (
        P(("groups", "inst"), None),
        P(("groups", "inst"), None),
        P(("groups", "inst"), None),
        P(("groups", "inst"), None, None, None, "tp", None),
        P(("groups", "inst"), None, None, "tp", None),
        P(("groups", "inst"), None, None, "tp", None),
        P(("groups", "inst")),
        P(("groups", "inst"), None),
        P(("groups", "inst"), None, "tp", None),
        P(("groups", "inst"), None, None, "tp", None),
    )
    return jax.shard_map(
        body,
        mesh=mesh,
        in_specs=placed,
        out_specs=P(("groups", "inst"), None, "tp", None),
        check_vma=False,
    )
```

time: 129 us -> 66.7 us (0.52)
  matrix products: 49.2 us -> 0 us
  Pallas kernels: 0 us -> 40.9 us
  other arithmetic: 25.3 us -> 0.15 us
  local copies, waits for them, and re-layouts: 21.1 us -> 5.29 us
  waiting for transfers between devices: 14.8 us -> 6.85 us
  starting transfers between devices: 17.7 us -> 12.5 us
    dot_general x8 -> x0, matrix products: 49.2 us -> none  [the longest x4 30.4 us: merge_block(): jnp.einsum(einsum_form, weights.astype(jnp.bfloat16), values, preferred_e...]
    pallas_call x0 -> x4, Pallas kernels: none -> 40.9 us  [the longest x1 19.7 us: tail_attention(): pl.pallas_call(functools.partial(tail_kernel, scale), grid=(tail_count //...]
    reduce_sum x5 -> x0, other arithmetic: 19.8 us -> none  [the longest x4 18.8 us: merge_block(): weight_sum = weight_sum * shrink + jnp.sum(weights, axis=-1)]
    all_to_all x3 -> x0, starting transfers between devices: 17.7 us -> none  [the longest x1 7.29 us: body(): lax.all_to_all(slot_out, 'inst', split_axis=0, concat_axis=0, tiled=True)]
    all_to_all x3 -> x0, waiting for transfers between devices: 14.8 us -> none  [the longest x1 12 us: body(): lax.all_to_all(outgoing, 'inst', split_axis=0, concat_axis=0, tiled=True)]
    ppermute x0 -> x7, starting transfers between devices: none -> 12.5 us  [body(): lax.ppermute(packed[k], 'inst', [(i, i ^ k) for i in range(members)])]
    scatter x5 -> x0, local copies, waits for them, and re-layouts: 7.66 us -> none  [the longest x1 2.5 us: body(): outgoing = jnp.zeros((members, PAIR) + page_shape, page_rows.dtype).at[ta...]
    ppermute x0 -> x7, waiting for transfers between devices: none -> 6.85 us  [body(): lax.ppermute(packed[k], 'inst', [(i, i ^ k) for i in range(members)])]
  transfers between devices with their start and end apart: 3 -> 7, of which waited for: 2 -> 2; matrix products, arithmetic and copies ran while one was open for 66% -> 2% of each run, Pallas kernels for 0% -> 31%
where the time goes in v1:
time: 66.7 us; the launch traced here: 66.5 us
  Pallas kernels  40.9 us (61%)
  starting transfers between devices  12.5 us (19%)
  waiting for transfers between devices  6.85 us (10%)
  local copies, waits for them, and re-layouts  5.29 us (8%)
  between operations  0.73 us (1%)
    pallas_call x1, Pallas kernels, tail_attention(): pl.pallas_call(functools.partial(tail_kernel, scale), grid=(tail_count //...  19.7 us
    pallas_call x1, Pallas kernels, pack(): pl.pallas_call(functools.partial(pack_kernel, split), out_shape=out_shape...  17.8 us
    ppermute x7, starting transfers between devices, body(): lax.ppermute(packed[k], 'inst', [(i, i ^ k) for i in range(members)])  12.5 us
    ppermute x7, waiting for transfers between devices, body(): lax.ppermute(packed[k], 'inst', [(i, i ^ k) for i in range(members)])  6.85 us
    unnamed x16, local copies, waits for them, and re-layouts  4.29 us
    pallas_call x1, Pallas kernels, page_attention(): pl.pallas_call(functools.partial(page_kernel, scale, slots, split), out_s...  2.74 us
  transfers between devices with their start and end apart: 7, of which 2 were waited for; matrix products, arithmetic and copies ran while one was open for 2% of the time, Pallas kernels for 31%

profile of v1, /device:TPU:0, one launch (start us, length us, event | category | flops | bytes accessed | tf_op | source)
XLA Modules:
  0.0 66.5 jit_solution(15500447096460556531)
XLA Ops:
  0.0 17.8 %pack_pages.1 = (bf16[528,128]{1,0:T(8,128)(2,1)}, bf16[528,128]{1,0:T(8,128)(2,1)}, bf16[528,128]{1,0:T(8,128)(2,1)}, bf16[528,128]{1,0:T(8,128)(2,1)}, bf16[52...) custom-call(s32[1]{0:T(128)} %bitcast.7.me_ref, ...), custom_call_target="tpu_custom_call" | custom-call | tf_op jit(solution)/shard_map/pack_pages/pallas_call | solution.py:133
  17.8 3.0 %collective-permute-start = (bf16[528,128]{1,0:T(8,128)(2,1)}, bf16[528,128]{1,0:T(8,128)(2,1)S(1)}, u32[]{:S(2)}, u32[]{:S(2)}) collective-permute-start(bf16[528,128]{1,0:T(8,128)(2,1)} %get-tuple-element.20), channel_id=1, source_target_pairs={{0,2},{2,0},{4,6},{6,4},{8,10},{10,8},{12,14},{14,12},{1,3},{3,1},... | collective-permute-start | bytes 405512 | tf_op jit(solution)/shard_map/ppermute | solution.py:396
  20.8 1.6 %collective-permute-start.1 = (bf16[528,128]{1,0:T(8,128)(2,1)}, bf16[528,128]{1,0:T(8,128)(2,1)S(1)}, u32[]{:S(2)}, u32[]{:S(2)}) collective-permute-start(bf16[528,128]{1,0:T(8,128)(2,1)} %get-tuple-element.21), channel_id=1, source_target_pairs={{0,4},{2,6},{4,0},{6,2},{8,12},{10,14},{12,8},{14,10},{1,5},{3,7},... | collective-permute-start | bytes 405512 | tf_op jit(solution)/shard_map/ppermute | solution.py:396
  22.3 0.0 collective-permute-start.2
  22.3 3.0 %collective-permute-start.3 = (bf16[528,128]{1,0:T(8,128)(2,1)}, bf16[528,128]{1,0:T(8,128)(2,1)S(1)}, u32[]{:S(2)}, u32[]{:S(2)}) collective-permute-start(bf16[528,128]{1,0:T(8,128)(2,1)} %get-tuple-element.23), channel_id=1, source_target_pairs={{0,8},{2,10},{4,12},{6,14},{8,0},{10,2},{12,4},{14,6},{1,9},{3,11}... | collective-permute-start | bytes 405512 | tf_op jit(solution)/shard_map/ppermute | solution.py:396
  25.3 1.3 %collective-permute-start.4 = (bf16[528,128]{1,0:T(8,128)(2,1)}, bf16[528,128]{1,0:T(8,128)(2,1)S(1)}, u32[]{:S(2)}, u32[]{:S(2)}) collective-permute-start(bf16[528,128]{1,0:T(8,128)(2,1)} %get-tuple-element.24), channel_id=1, source_target_pairs={{0,10},{2,8},{4,14},{6,12},{8,2},{10,0},{12,6},{14,4},{1,11},{3,9}... | collective-permute-start | bytes 405512 | tf_op jit(solution)/shard_map/ppermute | solution.py:396
  27.3 0.9 %slice_bitcast_fusion.q_ref = bf16[16,32,128]{2,1,0:T(8,128)(2,1)S(1)} fusion(bf16[1,272,32,128]{3,2,1,0:T(8,128)(2,1)} %q_ref.1), kind=kLoop, calls=%fused_computation | loop fusion | bytes 262144 | tf_op jit(solution)/shard_map/squeeze | solution.py:404
  28.2 0.0 copy-start.2
  28.2 1.6 %copy-done.2 = bf16[1,272,32,128]{3,2,1,0:T(8,128)(2,1)S(1)} copy-done((bf16[1,272,32,128]{3,2,1,0:T(8,128)(2,1)S(1)}, bf16[1,272,32,128]{3,2,1,0:T(8,128)(2,1)}, u32[]{:S(2)}) %copy-start.2) | copy-done | bytes 2228248
  29.8 0.0 copy-start.3
  29.8 1.1 %copy-done.3 = bf16[1,272,2,4,128]{4,3,2,1,0:T(4,128)(2,1)S(1)} copy-done((bf16[1,272,2,4,128]{4,3,2,1,0:T(4,128)(2,1)S(1)}, bf16[1,272,2,4,128]{4,3,2,1,0:T(4,128)(2,1)}, u32[]{:S(2)}) %copy-start.3) | copy-done | bytes 557080
  30.9 0.0 copy-start.4
  30.9 1.6 %copy-done.4 = bf16[1,1024,2,4,128]{4,3,2,1,0:T(4,128)(2,1)S(1)} copy-done((bf16[1,1024,2,4,128]{4,3,2,1,0:T(4,128)(2,1)S(1)}, bf16[1,1024,2,4,128]{4,3,2,1,0:T(4,128)(2,1)}, u32[]{:S(2)}) %copy-start.4) | copy-done | bytes 2097176
  32.5 0.0 copy-start.5
  32.5 0.0 copy-start.7
  32.5 0.0 copy-start.6
  32.5 0.0 copy-start.1
  32.5 0.0 copy-start
  32.5 19.7 %tail_attention.1.out_in = bf16[1,272,32,128]{3,2,1,0:T(8,128)(2,1)} custom-call(s32[1]{0:T(128)S(6)} %copy.13.prefix_ref, bf16[1,272,32,128]{3,2,1,0:T(8,128)(2,1)S(1)} %copy-done.2, bf16[8192,128]{1,0:T(8,128)(2,1)S(1)} %bitcast.14, bf16[2176,128]{1,0:T(8,128)(2,1)S(1)} %bitcast.13), custom_call_target="tpu_custom_call" | custom-call | flops 21474836480 | bytes 8388608 | tf_op jit(solution)/shard_map/tail_attention/pallas_call | solution.py:200
  52.2 0.0 copy-done.5
  52.2 0.1 iota_select_fusion
  52.3 0.0 collective-permute-done.refs_1_
  52.3 0.0 copy-done.7
  52.3 3.6 %collective-permute-start.5 = (bf16[528,128]{1,0:T(8,128)(2,1)S(1)}, bf16[528,128]{1,0:T(8,128)(2,1)S(1)}, u32[]{:S(2)}, u32[]{:S(2)}) collective-permute-start(bf16[528,128]{1,0:T(8,128)(2,1)S(1)} %copy-done.7), channel_id=1, source_target_pairs={{0,12},{2,14},{4,8},{6,10},{8,4},{10,6},{12,0},{14,2},{1,13},{3,15... | collective-permute-start | bytes 405512 | tf_op jit(solution)/shard_map/ppermute | solution.py:396
  55.9 0.0 collective-permute-done.1.refs_2_
  55.9 0.0 copy-done.6
  55.9 0.1 collective-permute-start.6
  56.0 0.1 select_n.9
  56.1 0.1 add_bitcast_fusion.code_ref
  56.2 0.0 copy-done.1
  56.2 0.7 %decode_local.1 = (f32[4,128,128]{2,1,0:T(8,128)S(1)}, f32[4,128,128]{2,1,0:T(8,128)S(1)}, f32[4,128,128]{2,1,0:T(8,128)S(1)}) custom-call(s32[1,80]{1,0:T(1,128)S(1)} %add_bitcast_fusion.code_ref, bf16[16,32,128]{2,1,0:T(8,128)(2,1)S(1)} %slice_bitcast_fusion.q_ref, bf16[512,128]{1,0:T(8,128)(2,1)S(1)} %bitcast.12, bf16[128,128]{1,0:T(8,128)(2,1)S(1)} %bitcast.11), custom_call_target="tpu_custom_call" | custom-call | flops 41943040 | bytes 3145728 | tf_op jit(solution)/shard_map/decode_local/pallas_call | solution.py:265
  56.9 0.0 collective-permute-done.2.refs_3_
  56.9 0.0 collective-permute-done.3.refs_4_
  56.9 0.0 collective-permute-done.4.refs_5_
  56.9 3.0 %collective-permute-done.5.refs_6_ = bf16[528,128]{1,0:T(8,128)(2,1)S(1)} collective-permute-done((bf16[528,128]{1,0:T(8,128)(2,1)S(1)}, bf16[528,128]{1,0:T(8,128)(2,1)S(1)}, u32[]{:S(2)}, u32[]{:S(2)}) %collective-permute-start.5) | collective-permute-done | bytes 135200 | tf_op jit(solution)/shard_map/ppermute | solution.py:396
  60.0 3.8 %collective-permute-done.6.refs_7_ = bf16[528,128]{1,0:T(8,128)(2,1)S(1)} collective-permute-done((bf16[528,128]{1,0:T(8,128)(2,1)S(1)}, bf16[528,128]{1,0:T(8,128)(2,1)S(1)}, u32[]{:S(2)}, u32[]{:S(2)}) %collective-permute-start.6) | collective-permute-done | bytes 135200 | tf_op jit(solution)/shard_map/ppermute | solution.py:396
  63.8 0.0 copy-done
  63.8 2.7 %decode_pages.1 = bf16[1,272,32,128]{3,2,1,0:T(8,128)(2,1)} custom-call(bf16[16,32,128]{2,1,0:T(8,128)(2,1)S(1)} %slice_bitcast_fusion.q_ref, f32[4,128,128]{2,1,0:T(8,128)S(1)} %get-tuple-element.16.m_ref, f32[4,128,128]{2,1,0:T(8,128)S(1)} %get-tuple-element.17.l_ref, f32[4,128,128]{2,1,0:T(8,128)S(1)} %get-tuple-element.18.a_ref, ...), custom_call_target="tpu_custom_call", output_to_operand_aliasing={{}: (4, {})} | custom-call | tf_op jit(solution)/shard_map/decode_pages/pallas_call | solution.py:352
  (2 shorter events, 0.0 us)
Async XLA Ops:
  17.8 34.5 %collective-permute-start = (bf16[528,128]{1,0:T(8,128)(2,1)}, bf16[528,128]{1,0:T(8,128)(2,1)S(1)}, u32[]{:S(2)}, u32[]{:S(2)}) collective-permute-start(bf16[528,128]{1,0:T(8,128)(2,1)} %get-tuple-element.20), channel_id=1, source_target_pairs={{0,2},{2,0},{4,6},{6,4},{8,10},{10,8},{12,14},{14,12},{1,3},{3,1},... | collective-permute-start | bytes 405512 | tf_op jit(solution)/shard_map/ppermute | solution.py:396
  20.8 35.2 %collective-permute-start.1 = (bf16[528,128]{1,0:T(8,128)(2,1)}, bf16[528,128]{1,0:T(8,128)(2,1)S(1)}, u32[]{:S(2)}, u32[]{:S(2)}) collective-permute-start(bf16[528,128]{1,0:T(8,128)(2,1)} %get-tuple-element.21), channel_id=1, source_target_pairs={{0,4},{2,6},{4,0},{6,2},{8,12},{10,14},{12,8},{14,10},{1,5},{3,7},... | collective-permute-start | bytes 405512 | tf_op jit(solution)/shard_map/ppermute | solution.py:396
  22.3 34.5 %collective-permute-start.2 = (bf16[528,128]{1,0:T(8,128)(2,1)}, bf16[528,128]{1,0:T(8,128)(2,1)S(1)}, u32[]{:S(2)}, u32[]{:S(2)}) collective-permute-start(bf16[528,128]{1,0:T(8,128)(2,1)} %get-tuple-element.22), channel_id=1, source_target_pairs={{0,6},{2,4},{4,2},{6,0},{8,14},{10,12},{12,10},{14,8},{1,7},{3,5},... | collective-permute-start | bytes 405512 | tf_op jit(solution)/shard_map/ppermute | solution.py:396
  22.3 34.5 %collective-permute-start.3 = (bf16[528,128]{1,0:T(8,128)(2,1)}, bf16[528,128]{1,0:T(8,128)(2,1)S(1)}, u32[]{:S(2)}, u32[]{:S(2)}) collective-permute-start(bf16[528,128]{1,0:T(8,128)(2,1)} %get-tuple-element.23), channel_id=1, source_target_pairs={{0,8},{2,10},{4,12},{6,14},{8,0},{10,2},{12,4},{14,6},{1,9},{3,11}... | collective-permute-start | bytes 405512 | tf_op jit(solution)/shard_map/ppermute | solution.py:396
  25.3 31.6 %collective-permute-start.4 = (bf16[528,128]{1,0:T(8,128)(2,1)}, bf16[528,128]{1,0:T(8,128)(2,1)S(1)}, u32[]{:S(2)}, u32[]{:S(2)}) collective-permute-start(bf16[528,128]{1,0:T(8,128)(2,1)} %get-tuple-element.24), channel_id=1, source_target_pairs={{0,10},{2,8},{4,14},{6,12},{8,2},{10,0},{12,6},{14,4},{1,11},{3,9}... | collective-permute-start | bytes 405512 | tf_op jit(solution)/shard_map/ppermute | solution.py:396
  28.2 1.6 %copy-start.2 = (bf16[1,272,32,128]{3,2,1,0:T(8,128)(2,1)S(1)}, bf16[1,272,32,128]{3,2,1,0:T(8,128)(2,1)}, u32[]{:S(2)}) copy-start(bf16[1,272,32,128]{3,2,1,0:T(8,128)(2,1)} %q_ref.1) | copy-start | bytes 6684676
  29.8 1.1 %copy-start.3 = (bf16[1,272,2,4,128]{4,3,2,1,0:T(4,128)(2,1)S(1)}, bf16[1,272,2,4,128]{4,3,2,1,0:T(4,128)(2,1)}, u32[]{:S(2)}) copy-start(bf16[1,272,2,4,128]{4,3,2,1,0:T(4,128)(2,1)} %param.19) | copy-start | bytes 1671172
  30.9 1.6 %copy-start.4 = (bf16[1,1024,2,4,128]{4,3,2,1,0:T(4,128)(2,1)S(1)}, bf16[1,1024,2,4,128]{4,3,2,1,0:T(4,128)(2,1)}, u32[]{:S(2)}) copy-start(bf16[1,1024,2,4,128]{4,3,2,1,0:T(4,128)(2,1)} %param.14) | copy-start | bytes 6291460
  32.5 19.8 %copy-start.5 = (s32[1,8]{1,0:T(1,128)S(1)}, s32[1,8]{1,0:T(1,128)}, u32[]{:S(2)}) copy-start(s32[1,8]{1,0:T(1,128)} %param.17) | copy-start | bytes 100
  32.5 19.8 %copy-start.7 = (bf16[528,128]{1,0:T(8,128)(2,1)S(1)}, bf16[528,128]{1,0:T(8,128)(2,1)}, u32[]{:S(2)}) copy-start(bf16[528,128]{1,0:T(8,128)(2,1)} %get-tuple-element.25) | copy-start | bytes 405508
  32.5 23.5 %copy-start.6 = (bf16[528,128]{1,0:T(8,128)(2,1)S(1)}, bf16[528,128]{1,0:T(8,128)(2,1)}, u32[]{:S(2)}) copy-start(bf16[528,128]{1,0:T(8,128)(2,1)} %get-tuple-element.26) | copy-start | bytes 405508
  32.5 23.7 %copy-start.1 = (bf16[1,64,2,4,128]{4,3,2,1,0:T(4,128)(2,1)S(1)}, bf16[1,64,2,4,128]{4,3,2,1,0:T(4,128)(2,1)}, u32[]{:S(2)}) copy-start(bf16[1,64,2,4,128]{4,3,2,1,0:T(4,128)(2,1)} %param.15) | copy-start | bytes 393220
  32.5 31.3 %copy-start = (bf16[528,128]{1,0:T(8,128)(2,1)S(1)}, bf16[528,128]{1,0:T(8,128)(2,1)}, u32[]{:S(2)}) copy-start(bf16[528,128]{1,0:T(8,128)(2,1)} %get-tuple-element.19.refs_0_) | copy-start | bytes 405508
  52.3 7.6 %collective-permute-start.5 = (bf16[528,128]{1,0:T(8,128)(2,1)S(1)}, bf16[528,128]{1,0:T(8,128)(2,1)S(1)}, u32[]{:S(2)}, u32[]{:S(2)}) collective-permute-start(bf16[528,128]{1,0:T(8,128)(2,1)S(1)} %copy-done.7), channel_id=1, source_target_pairs={{0,12},{2,14},{4,8},{6,10},{8,4},{10,6},{12,0},{14,2},{1,13},{3,15... | collective-permute-start | bytes 405512 | tf_op jit(solution)/shard_map/ppermute | solution.py:396
  55.9 7.8 %collective-permute-start.6 = (bf16[528,128]{1,0:T(8,128)(2,1)S(1)}, bf16[528,128]{1,0:T(8,128)(2,1)S(1)}, u32[]{:S(2)}, u32[]{:S(2)}) collective-permute-start(bf16[528,128]{1,0:T(8,128)(2,1)S(1)} %copy-done.6), channel_id=1, source_target_pairs={{0,14},{2,12},{4,10},{6,8},{8,6},{10,4},{12,2},{14,0},{1,15},{3,13... | collective-permute-start | bytes 405512 | tf_op jit(solution)/shard_map/ppermute | solution.py:396

commit v2 on v1

v2 whole, which is shorter than its diff:
```python
import functools
import math

import jax
import jax.numpy as jnp
from jax import lax
from jax.experimental import pallas as pl
from jax.experimental.pallas import tpu as pltpu
from jax.sharding import PartitionSpec as P

PAIR = 2
NEG = -1e30
F32 = jnp.float32
BF16 = jnp.bfloat16
META = 16
MIB = 1 << 20
LOW, HIGH = 2.0**-40, 2.0**120


def nt_dot(a, b):
    return lax.dot_general(a, b, (((1,), (1,)), ((), ())), preferred_element_type=F32)


def nn_dot(a, b):
    return jnp.dot(a, b, preferred_element_type=F32)


def unmix(kinds, rows):
    keys = rows // kinds
    i = lax.broadcasted_iota(jnp.int32, (rows, rows), 0)
    j = lax.broadcasted_iota(jnp.int32, (rows, rows), 1)
    return jnp.where(j == (i % keys) * kinds + i // keys, 1.0, 0.0).astype(BF16)


def scaled_queries(q, scale):
    q = q * scale
    high = q.astype(BF16)
    low = (q - high.astype(F32)).astype(BF16)
    return jnp.concatenate([high, low], axis=1)


def twice(k):
    return jnp.concatenate([k, k], axis=1)


def with_ones(v):
    return jnp.concatenate([v, jnp.ones_like(v)], axis=1)


def pack_kernel(split, me_ref, dest_hbm, slot_hbm, len_hbm, pages_hbm, *refs):
    *buffers, pages, dest, slot, length, count, table, small_sem, page_sem = refs
    requests, page_rows = pages.shape[:2]
    members = len(buffers) if split else buffers[0].shape[0]
    small = [
        pltpu.make_async_copy(source, target, small_sem.at[i])
        for i, (source, target) in enumerate(
            ((dest_hbm, dest), (slot_hbm, slot), (len_hbm, length))
        )
    ]
    large = pltpu.make_async_copy(pages_hbm, pages, page_sem)
    for copy in small:
        copy.start()
    large.start()

    def clear(k, _):
        count[k] = 0
        for half in range(PAIR):
            table[k * PAIR + half] = -1
        return 0

    lax.fori_loop(0, members, clear, 0)
    for copy in small:
        copy.wait()
    me = me_ref[0]

    def place(r, _):
        peer = dest[0, r] ^ me if split else dest[0, r]
        at = count[peer]
        count[peer] = at + 1
        table[peer * PAIR + at] = r
        return 0

    lax.fori_loop(0, requests, place, 0)
    lane = lax.broadcasted_iota(jnp.int32, (META, 128), 1)
    depth = 128 // (2 * PAIR)
    half_of, key_of = (lane // depth) % PAIR, lane % depth

    def fill(k, buffer):
        code = jnp.full((META, 128), -1.0, F32)
        for half in range(PAIR):
            r = table[k * PAIR + half]
            known = jnp.maximum(r, 0)
            live = jnp.where(r >= 0, length[0, known], 0)
            here = jnp.where(half_of == half, key_of, depth) < live
            code = jnp.where(here, slot[0, known].astype(F32), code)
            buffer[half * page_rows : (half + 1) * page_rows, :] = jnp.where(
                r >= 0, pages[known], jnp.zeros((page_rows, 128), BF16)
            )
        buffer[PAIR * page_rows : PAIR * page_rows + META, :] = code.astype(BF16)

    large.wait()
    if split:
        for k in range(members):
            fill(k, buffers[k])
    else:

        def fill_one(k, _):
            fill(k, buffers[0].at[k])
            return 0

        lax.fori_loop(0, members, fill_one, 0)


def pack(split, members, me, dest, slot, length, pages):
    requests, page_rows = pages.shape[:2]
    rows = PAIR * page_rows + META
    if split:
        out_shape = [jax.ShapeDtypeStruct((rows, 128), BF16)] * members
    else:
        out_shape = [jax.ShapeDtypeStruct((members, rows, 128), BF16)]
    return pl.pallas_call(
        functools.partial(pack_kernel, split),
        out_shape=out_shape,
        in_specs=[pl.BlockSpec(memory_space=pltpu.SMEM)] + [pl.BlockSpec(memory_space=pltpu.HBM)] * 4,
        out_specs=[pl.BlockSpec(memory_space=pltpu.VMEM)] * len(out_shape),
        scratch_shapes=[
            pltpu.VMEM(pages.shape, BF16),
            pltpu.SMEM((1, requests), jnp.int32),
            pltpu.SMEM((1, requests), jnp.int32),
            pltpu.SMEM((1, requests), jnp.int32),
            pltpu.SMEM((members,), jnp.int32),
            pltpu.SMEM((members * PAIR,), jnp.int32),
            pltpu.SemaphoreType.DMA((3,)),
            pltpu.SemaphoreType.DMA,
        ],
        compiler_params=pltpu.CompilerParams(vmem_limit_bytes=32 * MIB),
        name="pack_pages",
    )(me, *(pltpu.with_memory_space_constraint(a, pltpu.HBM) for a in (dest, slot, length, pages)))


def sort_rows(cache_ref, fresh_ref, prefix, keys, values_t):
    kv_heads, total, width = keys.shape
    kinds = 2 * kv_heads
    context = cache_ref.shape[0] // kinds
    order = unmix(kinds, 256)
    depth = 256 // kinds
    many = 4 * depth
    for at in range(0, total, many):
        source, base = (cache_ref, at) if at < context else (fresh_ref, at - context)
        parts = [source[base * kinds + 256 * i : base * kinds + 256 * (i + 1), :] for i in range(4)]
        done = nn_dot(order, jnp.concatenate(parts, axis=1))
        parts = [done[:, i * width : (i + 1) * width] for i in range(4)]
        limit = prefix if at < context else total
        live = at + lax.broadcasted_iota(jnp.int32, (many, width), 0) < limit
        for kind in range(kinds):
            rows = jnp.concatenate([p[kind * depth : (kind + 1) * depth] for p in parts], axis=0)
            rows = jnp.where(live, rows, 0.0).astype(BF16)
            if kind < kv_heads:
                keys[kind, at : at + many, :] = rows
            else:
                values_t[kind - kv_heads, 0:width, at : at + many] = rows.T
    extra = values_t.shape[1] - width
    lane = lax.broadcasted_iota(jnp.int32, (extra, total), 1)
    ones = jnp.where((lane < prefix) | (lane >= context), 1.0, 0.0).astype(BF16)
    for h in range(kv_heads):
        values_t[h, width:, :] = ones


def tail_kernel(scale, slots, near_count, prefix_ref, cached_ref, q_ref, step_q_ref, cache_ref, fresh_ref, own_ref, *refs):
    near = refs[:near_count]
    o_ref, scaled_ref, *state, keys, values_t, mixed, some_keys, some_values = refs[near_count:]
    block, heads, width = q_ref.shape[1:]
    kv_heads, total = keys.shape[:2]
    group = heads // kv_heads
    context = cache_ref.shape[0] // (2 * kv_heads)
    step = pl.program_id(0)
    prefix = prefix_ref[0]

    @pl.when(step == 0)
    def _():
        sort_rows(cache_ref, fresh_ref, prefix, keys, values_t)
        start_decode(
            scale, slots, cached_ref, step_q_ref, own_ref, fresh_ref, total - context, scaled_ref, state, some_keys, some_values
        )
        if near:
            add_pages(slots, group, near, scaled_ref, state, some_keys, some_values)

    rows = block * group
    queries = q_ref[0].astype(F32).reshape(block, kv_heads, group, width)

    def attend(at, exact):
        count = context + (at + 1) * block
        fine = jnp.ones((8, rows), F32)
        for h in range(kv_heads):
            q = scaled_queries(queries[:, h].reshape(rows, width), scale)
            scores = nt_dot(twice(keys[h, :count]), q)
            if exact:
                key = lax.broadcasted_iota(jnp.int32, (count, rows), 0)
                row = lax.broadcasted_iota(jnp.int32, (count, rows), 1) // group
                limit = jnp.where(key < context, prefix, row + (context + at * block + 1))
                scores = jnp.where(key < limit, scores, NEG)
                weights = jnp.exp2(scores - jnp.max(scores, axis=0, keepdims=True))
            else:
                weights = jnp.exp2(scores)
                key = lax.broadcasted_iota(jnp.int32, (block, rows), 0)
                row = lax.broadcasted_iota(jnp.int32, (block, rows), 1) // group
                last = jnp.where(key <= row, weights[count - block :], 0.0)
                weights = jnp.concatenate([weights[: count - block], last], axis=0)
            summed = nn_dot(values_t[h, :, :count], weights.astype(BF16))
            total_weight = summed[width : width + 8]
            fine = jnp.where(
                total_weight >= LOW, jnp.where(total_weight <= HIGH, fine, 0.0), 0.0
            )
            out = summed[:width] / total_weight[0:1]
            mixed[:, h] = out.T.reshape(block, group, width)
        return fine

    for at in range((total - context) // block):

        @pl.when(step == at)
        def _():
            fine = attend(at, False)

            @pl.when(jnp.min(fine) < 0.5)
            def _():
                attend(at, True)

    o_ref[0] = mixed[...].reshape(block, heads, width).astype(BF16)


def tail_attention(prefix, cached, queries, cache, fresh, own, near, tail_count, kv_heads):
    _, row_count, heads, width = queries.shape
    block = min(128, tail_count)
    context = cache.shape[0] // (2 * kv_heads)
    total = context + tail_count
    count = row_count - tail_count
    slots = cached.shape[1]
    rows = count * heads // kv_heads
    local = (own.shape[0] // (2 * kv_heads)) + count
    chunk = max(local, len(near) * PAIR * 32)
    scale = math.log2(math.e) / math.sqrt(width)
    spec = pl.BlockSpec((1, block, heads, width), lambda i: (0, i, 0, 0))
    step_spec = pl.BlockSpec((1, count, heads, width), lambda i: (0, tail_count // count, 0, 0))
    whole = lambda a: pl.BlockSpec(a.shape, lambda i: (0,) * len(a.shape))
    far = lambda a: pltpu.with_memory_space_constraint(a, pltpu.HBM)
    smem = pl.BlockSpec(memory_space=pltpu.SMEM)
    state = jax.ShapeDtypeStruct((kv_heads, rows, width), F32)
    scaled = jax.ShapeDtypeStruct((kv_heads, rows, 2 * width), BF16)
    return pl.pallas_call(
        functools.partial(tail_kernel, scale, slots, len(near)),
        grid=(tail_count // block,),
        out_shape=[jax.ShapeDtypeStruct(queries.shape, BF16), scaled, state, state, state],
        in_specs=[smem, smem, spec, step_spec, whole(cache), whole(fresh), whole(own)] + [whole(a) for a in near],
        out_specs=[spec, whole(scaled), whole(state), whole(state), whole(state)],
        scratch_shapes=[
            pltpu.VMEM((kv_heads, total, width), BF16),
            pltpu.VMEM((kv_heads, width + 16, total), BF16),
            pltpu.VMEM((block, kv_heads, heads // kv_heads, width), F32),
            pltpu.VMEM((kv_heads, chunk, width), BF16),
            pltpu.VMEM((kv_heads, chunk, width), BF16),
        ],
        compiler_params=pltpu.CompilerParams(vmem_limit_bytes=40 * MIB),
        cost_estimate=pl.CostEstimate(
            flops=4 * tail_count * heads * total * width * 4,
            bytes_accessed=8 * MIB,
            transcendentals=tail_count * heads * total,
        ),
        name="tail_attention",
    )(prefix, cached, far(queries), far(queries), far(cache), far(fresh), far(own), *near)


def row_place(rows, columns, group, slots):
    row = lax.broadcasted_iota(jnp.int32, (rows, columns), 0) // group
    return row % slots, row // slots


def split_rows(rows, base, keys, values):
    kv_heads = keys.shape[0]
    depth = rows.shape[0] // (2 * kv_heads)
    for h in range(kv_heads):
        keys[h, base : base + depth, :] = rows[h * depth : (h + 1) * depth]
        values[h, base : base + depth, :] = rows[(kv_heads + h) * depth : (kv_heads + h + 1) * depth]


def start_decode(scale, slots, cached_ref, q_ref, own_ref, fresh_ref, tail_count, scaled_ref, state, keys, values):
    count, heads, width = q_ref.shape[1:]
    kv_heads = keys.shape[0]
    group = heads // kv_heads
    kinds = 2 * kv_heads
    own_count = own_ref.shape[0] // kinds
    total = own_count + count
    chunk = min(256, own_ref.shape[0])
    order = unmix(kinds, chunk)
    for at in range(own_ref.shape[0] // chunk):
        rows = nn_dot(order, own_ref[at * chunk : (at + 1) * chunk, :]).astype(BF16)
        split_rows(rows, at * chunk // kinds, keys, values)
    chunk = min(256, count * kinds)
    order = unmix(kinds, chunk)
    for at in range(count * kinds // chunk):
        begin = tail_count * kinds + at * chunk
        rows = nn_dot(order, fresh_ref[begin : begin + chunk, :]).astype(BF16)
        split_rows(rows, own_count + at * chunk // kinds, keys, values)
    rows = count * group
    key = lax.broadcasted_iota(jnp.int32, (1, total), 1)
    depth = own_count // slots
    code = jnp.where(key < own_count, -1, (key - own_count) % slots)
    for s in range(slots):
        mine = jnp.where(key < own_count, key // depth, -1) == s
        code = jnp.where(mine & (key % depth < cached_ref[0, s]), s, code)
    since = jnp.where(key < own_count, 0, (key - own_count) // slots)
    slot, made = row_place(rows, total, group, slots)
    allowed = (code == slot) & (since <= made)
    queries = q_ref[0].astype(F32).reshape(count, kv_heads, group, width)
    peaks, sums, mixes = state
    for h in range(kv_heads):
        q = scaled_queries(queries[:, h].reshape(rows, width), scale)
        scaled_ref[h] = q
        scores = jnp.where(allowed, nt_dot(q, twice(keys[h, :total])), NEG)
        peak = jnp.max(scores, axis=1, keepdims=True)
        weights = jnp.exp2(scores - peak).astype(BF16)
        summed = nn_dot(weights, with_ones(values[h, :total]))
        peaks[h] = jnp.broadcast_to(peak, (rows, width))
        sums[h] = summed[:, width:]
        mixes[h] = summed[:, :width]


def add_pages(slots, group, buffers, scaled_ref, state, keys, values):
    kv_heads, rows, width = state[0].shape
    kinds = 2 * kv_heads
    page_rows = (buffers[0].shape[0] - META) // PAIR
    depth = page_rows // kinds
    order = unmix(kinds, page_rows)
    lane = lax.broadcasted_iota(jnp.int32, (1, 128), 1)
    codes = []
    for k, buffer in enumerate(buffers):
        both = [buffer[half * page_rows : (half + 1) * page_rows, :] for half in range(PAIR)]
        done = nn_dot(order, jnp.concatenate(both, axis=1)).astype(BF16)
        for half in range(PAIR):
            split_rows(
                done[:, half * width : (half + 1) * width], (PAIR * k + half) * depth, keys, values
            )
        codes.append(buffer[PAIR * page_rows : PAIR * page_rows + META, :].astype(F32)[0:1, :])
    code = jnp.concatenate(
        [jnp.where(lane < 64, codes[k], codes[k + 1]) for k in range(0, len(codes), 2)], axis=1
    )
    total = code.shape[1]
    slot, _ = row_place(rows, total, group, slots)
    allowed = code == slot.astype(F32)
    peaks, sums, mixes = state
    for h in range(kv_heads):
        old_peak = peaks[h]
        scores = jnp.where(allowed, nt_dot(scaled_ref[h], twice(keys[h, :total])), NEG)
        peak = jnp.maximum(old_peak, jnp.max(scores, axis=1, keepdims=True))
        weights = jnp.exp2(scores - peak[:, 0:1]).astype(BF16)
        summed = nn_dot(weights, with_ones(values[h, :total]))
        shrink = jnp.exp2(old_peak - peak)
        peaks[h] = peak
        sums[h] = sums[h] * shrink + summed[:, width:]
        mixes[h] = mixes[h] * shrink + summed[:, :width]


def page_kernel(slots, scaled_ref, m_in, l_in, a_in, out_in, *refs):
    *arrived, out_ref, peaks, sums, mixes, keys, values, mixed, staged, sem = refs
    count, kv_heads, group, width = mixed.shape
    state = (peaks, sums, mixes)
    for kept, given in zip(state, (m_in, l_in, a_in)):
        kept[...] = given[...]
    if len(arrived) > 1:
        add_pages(slots, group, arrived, scaled_ref, state, keys, values)
    else:
        buffers = arrived[0]
        per = keys.shape[1] // 64

        def some(i, _):
            part = [buffers.at[i * per + k] for k in range(per)]
            add_pages(slots, group, part, scaled_ref, state, keys, values)
            return 0

        lax.fori_loop(0, buffers.shape[0] // per, some, 0)
    for h in range(kv_heads):
        mixed[:, h] = (mixes[h] / sums[h]).reshape(count, group, width)
    staged[...] = mixed[...].reshape(staged.shape).astype(BF16)
    tail_count = out_ref.shape[1] - count
    copy = pltpu.make_async_copy(staged, out_ref.at[0, pl.ds(tail_count, count)], sem)
    copy.start()
    copy.wait()


def page_attention(scaled, state, out, arrived, slots):
    kv_heads, rows, width = state[0].shape
    heads = out.shape[2]
    group = heads // kv_heads
    count = rows // group
    chunk = 64 * (len(arrived) if len(arrived) > 1 else 8)
    vmem = pl.BlockSpec(memory_space=pltpu.VMEM)
    hbm = pl.BlockSpec(memory_space=pltpu.HBM)
    return pl.pallas_call(
        functools.partial(page_kernel, slots),
        out_shape=jax.ShapeDtypeStruct(out.shape, BF16),
        in_specs=[vmem] * 4 + [hbm] + [vmem] * len(arrived),
        out_specs=hbm,
        input_output_aliases={4: 0},
        scratch_shapes=[pltpu.VMEM(state[0].shape, F32)] * 3
        + [
            pltpu.VMEM((kv_heads, chunk, width), BF16),
            pltpu.VMEM((kv_heads, chunk, width), BF16),
            pltpu.VMEM((count, kv_heads, group, width), F32),
            pltpu.VMEM((count, heads, width), BF16),
            pltpu.SemaphoreType.DMA,
        ],
        compiler_params=pltpu.CompilerParams(vmem_limit_bytes=48 * MIB),
        name="decode_pages",
    )(scaled, *state, out, *arrived)


def body(
    request_dest,
    request_slot,
    page_len,
    page_rows,
    kv_cache,
    decode_cache,
    prefix_len,
    cached_len,
    queries,
    fresh_kv,
):
    members = lax.axis_size("inst")
    slots = cached_len.shape[1]
    row_count, heads, width = queries.shape[1:]
    kv_heads = kv_cache.shape[3]
    tail_count = row_count - 2 * slots
    requests, page_depth = page_rows.shape[1:3]
    split = members <= 8
    me = lax.axis_index("inst").astype(jnp.int32)

    pages = page_rows.reshape(requests, page_depth * 2 * kv_heads, width)
    packed = pack(split, members, me.reshape(1), request_dest, request_slot, page_len, pages)
    if split:
        half = members // 2
        swap = lambda block, k: lax.ppermute(block, "inst", [(i, i ^ k) for i in range(members)])
        near = [packed[0]] + [swap(packed[k], k) for k in range(1, half)]
        arrived = []
        for k in range(members - 1, half - 1, -1):
            arrived.append(swap(packed[k], k))
    else:
        near = []
        arrived = [lax.all_to_all(packed[0], "inst", split_axis=0, concat_axis=0, tiled=True)]

    out, scaled, *state = tail_attention(
        prefix_len,
        cached_len,
        queries,
        kv_cache.reshape(-1, width),
        fresh_kv.reshape(-1, width),
        decode_cache.reshape(-1, width),
        near,
        tail_count,
        kv_heads,
    )
    return page_attention(scaled, state, out, arrived, slots)


def solution(mesh):
    placed = (
        P(("groups", "inst"), None),
        P(("groups", "inst"), None),
        P(("groups", "inst"), None),
        P(("groups", "inst"), None, None, None, "tp", None),
        P(("groups", "inst"), None, None, "tp", None),
        P(("groups", "inst"), None, None, "tp", None),
        P(("groups", "inst")),
        P(("groups", "inst"), None),
        P(("groups", "inst"), None, "tp", None),
        P(("groups", "inst"), None, None, "tp", None),
    )
    return jax.shard_map(
        body,
        mesh=mesh,
        in_specs=placed,
        out_specs=P(("groups", "inst"), None, "tp", None),
        check_vma=False,
    )
```

time: 66.7 us -> 48.4 us (0.73)
  the two profiles are of different devices: /device:TPU:0 before, /device:TPU:28 now
where the time goes in v2:
time: 48.4 us; the launch traced here: 48.3 us
  Pallas kernels  33.5 us (69%)
  starting transfers between devices  11.3 us (23%)
  waiting for transfers between devices  2.13 us (4%)
  between operations  0.71 us (1%)
  local copies, waits for them, and re-layouts  0.66 us (1%)
    pallas_call x1, Pallas kernels, tail_attention(): pl.pallas_call(functools.partial(tail_kernel, scale, slots, len(near)), g...  29.9 us
    ppermute x7, starting transfers between devices, body(): lax.ppermute(block, 'inst', [(i, i ^ k) for i in range(members)])  11.3 us
    pallas_call x1, Pallas kernels, page_attention(): pl.pallas_call(functools.partial(page_kernel, slots), out_shape=jax.Shape...  2.24 us
    ppermute x7, waiting for transfers between devices, body(): lax.ppermute(block, 'inst', [(i, i ^ k) for i in range(members)])  2.13 us
    pallas_call x1, Pallas kernels, pack(): pl.pallas_call(functools.partial(pack_kernel, split), out_shape=out_shape...  1.33 us
  transfers between devices with their start and end apart: 7, of which 1 were waited for; matrix products, arithmetic and copies ran while one was open for 0% of the time, Pallas kernels for 62%

profile of v2, /device:TPU:28, one launch (start us, length us, event | category | flops | bytes accessed | tf_op | source)
XLA Modules:
  0.0 48.3 jit_solution(15795485329336167938)
XLA Ops:
  0.0 1.3 %pack_pages.1 = (bf16[528,128]{1,0:T(8,128)(2,1)S(1)}, bf16[528,128]{1,0:T(8,128)(2,1)S(1)}, bf16[528,128]{1,0:T(8,128)(2,1)S(1)}, bf16[528,128]{1,0:T(8,128)(2,...) custom-call(s32[1]{0:T(128)} %bitcast.3.me_ref, ...), custom_call_target="tpu_custom_call" | custom-call | tf_op jit(solution)/shard_map/pack_pages/pallas_call | solution.py:121
  1.3 0.6 %collective-permute-start = (bf16[528,128]{1,0:T(8,128)(2,1)S(1)}, bf16[528,128]{1,0:T(8,128)(2,1)S(1)}, u32[]{:S(2)}, u32[]{:S(2)}) collective-permute-start(bf16[528,128]{1,0:T(8,128)(2,1)S(1)} %get-tuple-element.19), channel_id=1, source_target_pairs={{0,2},{2,0},{4,6},{6,4},{8,10},{10,8},{12,14},{14,12},{1,3},{3,1},... | collective-permute-start | bytes 405512 | tf_op jit(solution)/shard_map/ppermute | solution.py:441
  1.9 0.4 collective-permute-start.1
  2.4 2.5 %collective-permute-start.2 = (bf16[528,128]{1,0:T(8,128)(2,1)S(1)}, bf16[528,128]{1,0:T(8,128)(2,1)S(1)}, u32[]{:S(2)}, u32[]{:S(2)}) collective-permute-start(bf16[528,128]{1,0:T(8,128)(2,1)S(1)} %get-tuple-element.21), channel_id=1, source_target_pairs={{0,6},{2,4},{4,2},{6,0},{8,14},{10,12},{12,10},{14,8},{1,7},{3,5},... | collective-permute-start | bytes 405512 | tf_op jit(solution)/shard_map/ppermute | solution.py:441
  4.9 0.0 collective-permute-start.3
  4.9 3.8 %collective-permute-start.4 = (bf16[528,128]{1,0:T(8,128)(2,1)S(1)}, bf16[528,128]{1,0:T(8,128)(2,1)S(1)}, u32[]{:S(2)}, u32[]{:S(2)}) collective-permute-start(bf16[528,128]{1,0:T(8,128)(2,1)S(1)} %get-tuple-element.28), channel_id=1, source_target_pairs={{0,12},{2,14},{4,8},{6,10},{8,4},{10,6},{12,0},{14,2},{1,13},{3,15... | collective-permute-start | bytes 405512 | tf_op jit(solution)/shard_map/ppermute | solution.py:441
  9.3 0.0 collective-permute-done.refs_1_
  9.3 0.1 collective-permute-start.5
  9.4 0.0 collective-permute-done.1.refs_2_
  9.4 3.9 %collective-permute-start.6 = (bf16[528,128]{1,0:T(8,128)(2,1)S(1)}, bf16[528,128]{1,0:T(8,128)(2,1)S(1)}, u32[]{:S(2)}, u32[]{:S(2)}) collective-permute-start(bf16[528,128]{1,0:T(8,128)(2,1)S(1)} %get-tuple-element.30), channel_id=1, source_target_pairs={{0,8},{2,10},{4,12},{6,14},{8,0},{10,2},{12,4},{14,6},{1,9},{3,11}... | collective-permute-start | bytes 405512 | tf_op jit(solution)/shard_map/ppermute | solution.py:441
  13.3 2.1 %collective-permute-done.2.refs_3_ = bf16[528,128]{1,0:T(8,128)(2,1)S(1)} collective-permute-done((bf16[528,128]{1,0:T(8,128)(2,1)S(1)}, bf16[528,128]{1,0:T(8,128)(2,1)S(1)}, u32[]{:S(2)}, u32[]{:S(2)}) %collective-permute-start.2) | collective-permute-done | bytes 135200 | tf_op jit(solution)/shard_map/ppermute | solution.py:441
  15.4 0.0 copy-start
  15.4 0.7 %copy-done = s32[1,8]{1,0:T(1,128)S(1)} copy-done((s32[1,8]{1,0:T(1,128)S(1)}, s32[1,8]{1,0:T(1,128)}, u32[]{:S(2)}) %copy-start) | copy-done | bytes 56
  16.0 29.9 %tail_attention.1 = (bf16[1,272,32,128]{3,2,1,0:T(8,128)(2,1)}, bf16[4,128,256]{2,1,0:T(8,128)(2,1)S(1)}, f32[4,128,128]{2,1,0:T(8,128)S(1)}, f32[4,128,128]{2,1,0:T(8,128)S(1)}, f32[4,128,128]{2,1,0:T(8,128)S(1)}) custom-call(s32[1]{0:T(128)S(6)} %copy.13.prefix_ref, s32[1,8]{1,0:T(1,128)S(1)} %copy-done, bf16[1,272,32,128]{3,2,1,0:T(8,128)(2,1)} %step_q_ref.1, ...), custom_call_target="tpu_custom_call" | custom-call | flops 21474836480 | bytes 8388608 | tf_op jit(solution)/shard_map/tail_attention/pallas_call | solution.py:249
  46.0 0.0 collective-permute-done.3.refs_0_
  46.0 0.0 collective-permute-done.4.refs_1_
  46.0 0.0 collective-permute-done.5.refs_2_
  46.0 0.0 collective-permute-done.6.refs_3_
  46.0 2.2 %decode_pages.1 = bf16[1,272,32,128]{3,2,1,0:T(8,128)(2,1)} custom-call(bf16[4,128,256]{2,1,0:T(8,128)(2,1)S(1)} %get-tuple-element.22.scaled_ref, f32[4,128,128]{2,1,0:T(8,128)S(1)} %get-tuple-element.23.m_in, f32[4,128,128]{2,1,0:T(8,128)S(1)} %get-tuple-element.24.l_in, ...), custom_call_target="tpu_custom_call", output_to_operand_aliasing={{}: (4, {})} | custom-call | tf_op jit(solution)/shard_map/decode_pages/pallas_call | solution.py:397
Async XLA Ops:
  1.3 8.0 %collective-permute-start = (bf16[528,128]{1,0:T(8,128)(2,1)S(1)}, bf16[528,128]{1,0:T(8,128)(2,1)S(1)}, u32[]{:S(2)}, u32[]{:S(2)}) collective-permute-start(bf16[528,128]{1,0:T(8,128)(2,1)S(1)} %get-tuple-element.19), channel_id=1, source_target_pairs={{0,2},{2,0},{4,6},{6,4},{8,10},{10,8},{12,14},{14,12},{1,3},{3,1},... | collective-permute-start | bytes 405512 | tf_op jit(solution)/shard_map/ppermute | solution.py:441
  1.9 7.5 %collective-permute-start.1 = (bf16[528,128]{1,0:T(8,128)(2,1)S(1)}, bf16[528,128]{1,0:T(8,128)(2,1)S(1)}, u32[]{:S(2)}, u32[]{:S(2)}) collective-permute-start(bf16[528,128]{1,0:T(8,128)(2,1)S(1)} %get-tuple-element.20), channel_id=1, source_target_pairs={{0,4},{2,6},{4,0},{6,2},{8,12},{10,14},{12,8},{14,10},{1,5},{3,7},... | collective-permute-start | bytes 405512 | tf_op jit(solution)/shard_map/ppermute | solution.py:441
  2.4 13.0 %collective-permute-start.2 = (bf16[528,128]{1,0:T(8,128)(2,1)S(1)}, bf16[528,128]{1,0:T(8,128)(2,1)S(1)}, u32[]{:S(2)}, u32[]{:S(2)}) collective-permute-start(bf16[528,128]{1,0:T(8,128)(2,1)S(1)} %get-tuple-element.21), channel_id=1, source_target_pairs={{0,6},{2,4},{4,2},{6,0},{8,14},{10,12},{12,10},{14,8},{1,7},{3,5},... | collective-permute-start | bytes 405512 | tf_op jit(solution)/shard_map/ppermute | solution.py:441
  4.9 41.1 %collective-permute-start.3 = (bf16[528,128]{1,0:T(8,128)(2,1)S(1)}, bf16[528,128]{1,0:T(8,128)(2,1)S(1)}, u32[]{:S(2)}, u32[]{:S(2)}) collective-permute-start(bf16[528,128]{1,0:T(8,128)(2,1)S(1)} %get-tuple-element.27), channel_id=1, source_target_pairs={{0,14},{2,12},{4,10},{6,8},{8,6},{10,4},{12,2},{14,0},{1,15},{3,13... | collective-permute-start | bytes 405512 | tf_op jit(solution)/shard_map/ppermute | solution.py:441
  4.9 41.1 %collective-permute-start.4 = (bf16[528,128]{1,0:T(8,128)(2,1)S(1)}, bf16[528,128]{1,0:T(8,128)(2,1)S(1)}, u32[]{:S(2)}, u32[]{:S(2)}) collective-permute-start(bf16[528,128]{1,0:T(8,128)(2,1)S(1)} %get-tuple-element.28), channel_id=1, source_target_pairs={{0,12},{2,14},{4,8},{6,10},{8,4},{10,6},{12,0},{14,2},{1,13},{3,15... | collective-permute-start | bytes 405512 | tf_op jit(solution)/shard_map/ppermute | solution.py:441
  9.3 36.7 %collective-permute-start.5 = (bf16[528,128]{1,0:T(8,128)(2,1)S(1)}, bf16[528,128]{1,0:T(8,128)(2,1)S(1)}, u32[]{:S(2)}, u32[]{:S(2)}) collective-permute-start(bf16[528,128]{1,0:T(8,128)(2,1)S(1)} %get-tuple-element.29), channel_id=1, source_target_pairs={{0,10},{2,8},{4,14},{6,12},{8,2},{10,0},{12,6},{14,4},{1,11},{3,9}... | collective-permute-start | bytes 405512 | tf_op jit(solution)/shard_map/ppermute | solution.py:441
  9.4 36.6 %collective-permute-start.6 = (bf16[528,128]{1,0:T(8,128)(2,1)S(1)}, bf16[528,128]{1,0:T(8,128)(2,1)S(1)}, u32[]{:S(2)}, u32[]{:S(2)}) collective-permute-start(bf16[528,128]{1,0:T(8,128)(2,1)S(1)} %get-tuple-element.30), channel_id=1, source_target_pairs={{0,8},{2,10},{4,12},{6,14},{8,0},{10,2},{12,4},{14,6},{1,9},{3,11}... | collective-permute-start | bytes 405512 | tf_op jit(solution)/shard_map/ppermute | solution.py:441
  15.4 0.7 %copy-start = (s32[1,8]{1,0:T(1,128)S(1)}, s32[1,8]{1,0:T(1,128)}, u32[]{:S(2)}) copy-start(s32[1,8]{1,0:T(1,128)} %cached_ref.1) | copy-start | bytes 100

commit v3 on v2

--- a/solution.py
+++ b/solution.py
@@ -138,135 +138,202 @@
     )(me, *(pltpu.with_memory_space_constraint(a, pltpu.HBM) for a in (dest, slot, length, pages)))
 
 
-def sort_rows(cache_ref, fresh_ref, prefix, keys, values_t):
+def sort_some(at, source, order, limit, keys, values_t):
+    kv_heads, _, width = keys.shape
+    kinds = 2 * kv_heads
+    depth = 256 // kinds
+    many = source.shape[0] // kinds
+    parts = [source[256 * i : 256 * (i + 1), :] for i in range(many // depth)]
+    done = nn_dot(order, jnp.concatenate(parts, axis=1))
+    parts = [done[:, i * width : (i + 1) * width] for i in range(len(parts))]
+    live = at + lax.broadcasted_iota(jnp.int32, (many, width), 0) < limit
+    for kind in range(kinds):
+        rows = jnp.concatenate([p[kind * depth : (kind + 1) * depth] for p in parts], axis=0)
+        rows = jnp.where(live, rows, 0.0).astype(BF16)
+        if kind < kv_heads:
+            keys[kind, at : at + many, :] = rows
+        else:
+            values_t[kind - kv_heads, 0:width, at : at + many] = rows.T
+
+
+def attend(scale, at, exact, context, prefix, q_ref, keys, values_t, mixed, staged, out_ref, sems):
+    kv_heads, block, group, width = mixed.shape
+    rows = block * group
+    count = context + (at + 1) * block
+    here = pl.ds(at * block, block)
+    fine = jnp.ones((8, rows), F32)
+    copies = []
+    for h in range(kv_heads):
+        q = q_ref[0, here, h * group : (h + 1) * group, :].astype(F32).reshape(rows, width)
+        scores = nt_dot(twice(keys[h, :count]), scaled_queries(q, scale))
+        key = lax.broadcasted_iota(jnp.int32, (block, rows), 0)
+        row = lax.broadcasted_iota(jnp.int32, (block, rows), 1) // group
+        if exact:
+            dead = lax.broadcasted_iota(jnp.int32, (context, rows), 0) >= prefix
+            first = jnp.where(dead, NEG, scores[:context])
+            last = jnp.where(key <= row, scores[count - block :], NEG)
+            middle = [scores[context : count - block]] if at else []
+            scores = jnp.concatenate([first, *middle, last], axis=0)
+            weights = jnp.exp2(scores - jnp.max(scores, axis=0, keepdims=True))
+        else:
+            weights = jnp.exp2(scores)
+            last = jnp.where(key <= row, weights[count - block :], 0.0)
+            weights = jnp.concatenate([weights[: count - block], last], axis=0)
+        summed = nn_dot(values_t[h, :, :count], weights.astype(BF16))
+        total_weight = summed[width : width + 8]
+        fine = jnp.where(total_weight >= LOW, jnp.where(total_weight <= HIGH, fine, 0.0), 0.0)
+        mixed[h] = (summed[:width] / total_weight[0:1]).T.reshape(block, group, width)
+        if h % 2:
+            some = pl.ds((h - 1) * group, 2 * group)
+            staged[here, some, :] = jnp.concatenate([mixed[h - 1], mixed[h]], axis=1).astype(BF16)
+            copies.append(
+                pltpu.make_async_copy(
+                    staged.at[here, some, :], out_ref.at[0, here, some, :], sems.at[at, h // 2]
+                )
+            )
+            copies[-1].start()
+    return fine, copies
+
+
+def sort_kernel(scale, slots, prefix_ref, cached_hbm, q_hbm, cache_hbm, fresh_hbm, own_hbm, *refs):
+    keys, values_t, scaled_ref, *state = refs[:6]
+    some_keys, some_values, cached, step_q, cache, fresh, own, in_sems, sems = refs[6:]
+    count = step_q.shape[0]
     kv_heads, total, width = keys.shape
     kinds = 2 * kv_heads
-    context = cache_ref.shape[0] // kinds
+    context = cache.shape[0] // kinds
+    tail_count = total - context
+    prefix = prefix_ref[0]
+    many = 128 * kinds
+    loads = []
+    for i in range(in_sems.shape[0]):
+        size = cache.shape[0] // in_sems.shape[0]
+        part = pl.ds(i * size, size)
+        loads.append(pltpu.make_async_copy(cache_hbm.at[part, :], cache.at[part, :], in_sems.at[i]))
+    others = [
+        pltpu.make_async_copy(fresh_hbm, fresh, sems.at[0]),
+        pltpu.make_async_copy(own_hbm, own, sems.at[1]),
+        pltpu.make_async_copy(q_hbm.at[0, pl.ds(tail_count, count)], step_q, sems.at[2]),
+    ]
+    others.append(pltpu.make_async_copy(cached_hbm, cached, sems.at[3]))
+    for copy in others + loads:
+        copy.start()
     order = unmix(kinds, 256)
-    depth = 256 // kinds
-    many = 4 * depth
-    for at in range(0, total, many):
-        source, base = (cache_ref, at) if at < context else (fresh_ref, at - context)
-        parts = [source[base * kinds + 256 * i : base * kinds + 256 * (i + 1), :] for i in range(4)]
-        done = nn_dot(order, jnp.concatenate(parts, axis=1))
-        parts = [done[:, i * width : (i + 1) * width] for i in range(4)]
-        limit = prefix if at < context else total
-        live = at + lax.broadcasted_iota(jnp.int32, (many, width), 0) < limit
-        for kind in range(kinds):
-            rows = jnp.concatenate([p[kind * depth : (kind + 1) * depth] for p in parts], axis=0)
-            rows = jnp.where(live, rows, 0.0).astype(BF16)
-            if kind < kv_heads:
-                keys[kind, at : at + many, :] = rows
-            else:
-                values_t[kind - kv_heads, 0:width, at : at + many] = rows.T
     extra = values_t.shape[1] - width
     lane = lax.broadcasted_iota(jnp.int32, (extra, total), 1)
     ones = jnp.where((lane < prefix) | (lane >= context), 1.0, 0.0).astype(BF16)
     for h in range(kv_heads):
         values_t[h, width:, :] = ones
-
-
-def tail_kernel(scale, slots, near_count, prefix_ref, cached_ref, q_ref, step_q_ref, cache_ref, fresh_ref, own_ref, *refs):
-    near = refs[:near_count]
-    o_ref, scaled_ref, *state, keys, values_t, mixed, some_keys, some_values = refs[near_count:]
-    block, heads, width = q_ref.shape[1:]
-    kv_heads, total = keys.shape[:2]
-    group = heads // kv_heads
-    context = cache_ref.shape[0] // (2 * kv_heads)
-    step = pl.program_id(0)
-    prefix = prefix_ref[0]
-
-    @pl.when(step == 0)
-    def _():
-        sort_rows(cache_ref, fresh_ref, prefix, keys, values_t)
-        start_decode(
-            scale, slots, cached_ref, step_q_ref, own_ref, fresh_ref, total - context, scaled_ref, state, some_keys, some_values
+    for copy in others:
+        copy.wait()
+    start_decode(
+        scale, slots, cached, step_q, own, fresh, tail_count, scaled_ref, state, some_keys, some_values
+    )
+    for i in range(tail_count // 128):
+        sort_some(
+            context + i * 128, fresh.at[pl.ds(i * many, many), :], order, total, keys, values_t
         )
-        if near:
-            add_pages(slots, group, near, scaled_ref, state, some_keys, some_values)
-
-    rows = block * group
-    queries = q_ref[0].astype(F32).reshape(block, kv_heads, group, width)
-
-    def attend(at, exact):
-        count = context + (at + 1) * block
-        fine = jnp.ones((8, rows), F32)
-        for h in range(kv_heads):
-            q = scaled_queries(queries[:, h].reshape(rows, width), scale)
-            scores = nt_dot(twice(keys[h, :count]), q)
-            if exact:
-                key = lax.broadcasted_iota(jnp.int32, (count, rows), 0)
-                row = lax.broadcasted_iota(jnp.int32, (count, rows), 1) // group
-                limit = jnp.where(key < context, prefix, row + (context + at * block + 1))
-                scores = jnp.where(key < limit, scores, NEG)
-                weights = jnp.exp2(scores - jnp.max(scores, axis=0, keepdims=True))
-            else:
-                weights = jnp.exp2(scores)
-                key = lax.broadcasted_iota(jnp.int32, (block, rows), 0)
-                row = lax.broadcasted_iota(jnp.int32, (block, rows), 1) // group
-                last = jnp.where(key <= row, weights[count - block :], 0.0)
-                weights = jnp.concatenate([weights[: count - block], last], axis=0)
-            summed = nn_dot(values_t[h, :, :count], weights.astype(BF16))
-            total_weight = summed[width : width + 8]
-            fine = jnp.where(
-                total_weight >= LOW, jnp.where(total_weight <= HIGH, fine, 0.0), 0.0
-            )
-            out = summed[:width] / total_weight[0:1]
-            mixed[:, h] = out.T.reshape(block, group, width)
-        return fine
-
-    for at in range((total - context) // block):
-
-        @pl.when(step == at)
-        def _():
-            fine = attend(at, False)
-
-            @pl.when(jnp.min(fine) < 0.5)
-            def _():
-                attend(at, True)
-
-    o_ref[0] = mixed[...].reshape(block, heads, width).astype(BF16)
-
-
-def tail_attention(prefix, cached, queries, cache, fresh, own, near, tail_count, kv_heads):
+    per = context // 128 // len(loads)
+    for i in range(context // 128):
+        if i % per == 0:
+            loads[i // per].wait()
+        sort_some(i * 128, cache.at[pl.ds(i * many, many), :], order, prefix, keys, values_t)
+
+
+def far_off(a):
+    return pltpu.with_memory_space_constraint(a, pltpu.HBM)
+
+
+def sort_keys(prefix, cached, queries, cache, fresh, own, tail_count, kv_heads):
     _, row_count, heads, width = queries.shape
-    block = min(128, tail_count)
-    context = cache.shape[0] // (2 * kv_heads)
+    kinds = 2 * kv_heads
+    context = cache.shape[0] // kinds
     total = context + tail_count
     count = row_count - tail_count
-    slots = cached.shape[1]
     rows = count * heads // kv_heads
-    local = (own.shape[0] // (2 * kv_heads)) + count
-    chunk = max(local, len(near) * PAIR * 32)
+    local = own.shape[0] // kinds + count
     scale = math.log2(math.e) / math.sqrt(width)
-    spec = pl.BlockSpec((1, block, heads, width), lambda i: (0, i, 0, 0))
-    step_spec = pl.BlockSpec((1, count, heads, width), lambda i: (0, tail_count // count, 0, 0))
-    whole = lambda a: pl.BlockSpec(a.shape, lambda i: (0,) * len(a.shape))
-    far = lambda a: pltpu.with_memory_space_constraint(a, pltpu.HBM)
     smem = pl.BlockSpec(memory_space=pltpu.SMEM)
+    vmem = pl.BlockSpec(memory_space=pltpu.VMEM)
+    hbm = pl.BlockSpec(memory_space=pltpu.HBM)
     state = jax.ShapeDtypeStruct((kv_heads, rows, width), F32)
-    scaled = jax.ShapeDtypeStruct((kv_heads, rows, 2 * width), BF16)
     return pl.pallas_call(
-        functools.partial(tail_kernel, scale, slots, len(near)),
-        grid=(tail_count // block,),
-        out_shape=[jax.ShapeDtypeStruct(queries.shape, BF16), scaled, state, state, state],
-        in_specs=[smem, smem, spec, step_spec, whole(cache), whole(fresh), whole(own)] + [whole(a) for a in near],
-        out_specs=[spec, whole(scaled), whole(state), whole(state), whole(state)],
+        functools.partial(sort_kernel, scale, cached.shape[1]),
+        out_shape=[
+            jax.ShapeDtypeStruct((kv_heads, total, width), BF16),
+            jax.ShapeDtypeStruct((kv_heads, width + 16, total), BF16),
+            jax.ShapeDtypeStruct((kv_heads, rows, 2 * width), BF16),
+            state,
+            state,
+            state,
+        ],
+        in_specs=[smem, hbm, hbm, hbm, hbm, hbm],
+        out_specs=[vmem] * 6,
         scratch_shapes=[
-            pltpu.VMEM((kv_heads, total, width), BF16),
-            pltpu.VMEM((kv_heads, width + 16, total), BF16),
-            pltpu.VMEM((block, kv_heads, heads // kv_heads, width), F32),
-            pltpu.VMEM((kv_heads, chunk, width), BF16),
-            pltpu.VMEM((kv_heads, chunk, width), BF16),
+            pltpu.VMEM((kv_heads, local, width), BF16),
+            pltpu.VMEM((kv_heads, local, width), BF16),
+            pltpu.SMEM(cached.shape, jnp.int32),
+            pltpu.VMEM((count, heads, width), BF16),
+            pltpu.VMEM(cache.shape, BF16),
+            pltpu.VMEM(fresh.shape, BF16),
+            pltpu.VMEM(own.shape, BF16),
+            pltpu.SemaphoreType.DMA((1,)),
+            pltpu.SemaphoreType.DMA((4,)),
         ],
-        compiler_params=pltpu.CompilerParams(vmem_limit_bytes=40 * MIB),
+        compiler_params=pltpu.CompilerParams(vmem_limit_bytes=24 * MIB),
+        cost_estimate=pl.CostEstimate(flops=1, bytes_accessed=12 * MIB, transcendentals=0),
+        name="sort_keys",
+    )(prefix, *(far_off(a) for a in (cached, queries, cache, fresh, own)))
+
+
+def tail_kernel(scale, context, prefix_ref, q_ref, keys, values_t, out_ref, mixed, staged, sems):
+    block = mixed.shape[1]
+    prefix = prefix_ref[0]
+    results = []
+    for at in range(staged.shape[0] // block):
+        results.append(
+            attend(scale, at, False, context, prefix, q_ref, keys, values_t, mixed, staged, out_ref, sems)
+        )
+    for at, (fine, copies) in enumerate(results):
+        for copy in copies:
+            copy.wait()
+
+        @pl.when(jnp.min(fine) < 0.5)
+        def _():
+            _, again = attend(
+                scale, at, True, context, prefix, q_ref, keys, values_t, mixed, staged, out_ref, sems
+            )
+            for copy in again:
+                copy.wait()
+
+
+def tail_attention(prefix, queries, keys, values_t, tail_count):
+    _, row_count, heads, width = queries.shape
+    kv_heads, total, _ = keys.shape
+    block = min(128, tail_count)
+    group = heads // kv_heads
+    scale = math.log2(math.e) / math.sqrt(width)
+    smem = pl.BlockSpec(memory_space=pltpu.SMEM)
+    vmem = pl.BlockSpec(memory_space=pltpu.VMEM)
+    hbm = pl.BlockSpec(memory_space=pltpu.HBM)
+    return pl.pallas_call(
+        functools.partial(tail_kernel, scale, total - tail_count),
+        out_shape=jax.ShapeDtypeStruct(queries.shape, BF16),
+        in_specs=[smem] + [vmem] * 3,
+        out_specs=hbm,
+        scratch_shapes=[
+            pltpu.VMEM((kv_heads, block, group, width), F32),
+            pltpu.VMEM((tail_count, heads, width), BF16),
+            pltpu.SemaphoreType.DMA((tail_count // block, kv_heads // 2)),
+        ],
+        compiler_params=pltpu.CompilerParams(vmem_limit_bytes=36 * MIB),
         cost_estimate=pl.CostEstimate(
-            flops=4 * tail_count * heads * total * width * 4,
+            flops=16 * tail_count * heads * total * width,
             bytes_accessed=8 * MIB,
             transcendentals=tail_count * heads * total,
         ),
         name="tail_attention",
-    )(prefix, cached, far(queries), far(queries), far(cache), far(fresh), far(own), *near)
+    )(prefix, queries, keys, values_t)
 
 
 def row_place(rows, columns, group, slots):
@@ -283,7 +350,7 @@
 
 
 def start_decode(scale, slots, cached_ref, q_ref, own_ref, fresh_ref, tail_count, scaled_ref, state, keys, values):
-    count, heads, width = q_ref.shape[1:]
+    count, heads, width = q_ref.shape
     kv_heads = keys.shape[0]
     group = heads // kv_heads
     kinds = 2 * kv_heads
@@ -310,7 +377,7 @@
     since = jnp.where(key < own_count, 0, (key - own_count) // slots)
     slot, made = row_place(rows, total, group, slots)
     allowed = (code == slot) & (since <= made)
-    queries = q_ref[0].astype(F32).reshape(count, kv_heads, group, width)
+    queries = q_ref[...].astype(F32).reshape(count, kv_heads, group, width)
     peaks, sums, mixes = state
     for h in range(kv_heads):
         q = scaled_queries(queries[:, h].reshape(rows, width), scale)
@@ -324,7 +391,7 @@
         mixes[h] = summed[:, :width]
 
 
-def add_pages(slots, group, buffers, scaled_ref, state, keys, values):
+def add_pages(slots, group, buffers, scaled_ref, state, finish, keys, values, target=None):
     kv_heads, rows, width = state[0].shape
     kinds = 2 * kv_heads
     page_rows = (buffers[0].shape[0] - META) // PAIR
@@ -354,36 +421,74 @@
         weights = jnp.exp2(scores - peak[:, 0:1]).astype(BF16)
         summed = nn_dot(weights, with_ones(values[h, :total]))
         shrink = jnp.exp2(old_peak - peak)
-        peaks[h] = peak
-        sums[h] = sums[h] * shrink + summed[:, width:]
-        mixes[h] = mixes[h] * shrink + summed[:, :width]
+        weight_sum = sums[h] * shrink + summed[:, width:]
+        mix = mixes[h] * shrink + summed[:, :width]
+        if finish:
+            finish(h, weight_sum, mix)
+        else:
+            for kept, new in zip(target or state, (peak, weight_sum, mix)):
+                kept[h] = new
+
+
+def middle_kernel(slots, group, scaled_ref, m_in, l_in, a_in, *refs):
+    *arrived, peaks, sums, mixes, keys, values = refs
+    given, state = (m_in, l_in, a_in), (peaks, sums, mixes)
+    add_pages(slots, group, arrived, scaled_ref, given, None, keys, values, state)
+
+
+def middle_pages(scaled, state, arrived, slots, group):
+    kv_heads, rows, width = state[0].shape
+    vmem = pl.BlockSpec(memory_space=pltpu.VMEM)
+    return pl.pallas_call(
+        functools.partial(middle_kernel, slots, group),
+        out_shape=[jax.ShapeDtypeStruct(state[0].shape, F32)] * 3,
+        in_specs=[vmem] * (4 + len(arrived)),
+        out_specs=[vmem] * 3,
+        scratch_shapes=[pltpu.VMEM((kv_heads, 64 * len(arrived), width), BF16)] * 2,
+        compiler_params=pltpu.CompilerParams(vmem_limit_bytes=16 * MIB),
+        name="middle_pages",
+    )(scaled, *state, *arrived)
 
 
 def page_kernel(slots, scaled_ref, m_in, l_in, a_in, out_in, *refs):
-    *arrived, out_ref, peaks, sums, mixes, keys, values, mixed, staged, sem = refs
-    count, kv_heads, group, width = mixed.shape
-    state = (peaks, sums, mixes)
-    for kept, given in zip(state, (m_in, l_in, a_in)):
-        kept[...] = given[...]
+    *arrived, out_ref, peaks, sums, mixes, keys, values, mixed, staged, sems = refs
+    kv_heads, count, group, width = mixed.shape
+    given, state = (m_in, l_in, a_in), (peaks, sums, mixes)
+    tail_count = out_ref.shape[1] - count
+    copies = []
+
+    def finish(h, weight_sum, mix):
+        mixed[h] = (mix / weight_sum).reshape(count, group, width)
+        if h % 2:
+            some = pl.ds((h - 1) * group, 2 * group)
+            staged[:, some, :] = jnp.concatenate([mixed[h - 1], mixed[h]], axis=1).astype(BF16)
+            copies.append(
+                pltpu.make_async_copy(
+                    staged.at[:, some, :],
+                    out_ref.at[0, pl.ds(tail_count, count), some, :],
+                    sems.at[h // 2],
+                )
+            )
+            copies[-1].start()
+
     if len(arrived) > 1:
-        add_pages(slots, group, arrived, scaled_ref, state, keys, values)
+        add_pages(slots, group, arrived, scaled_ref, given, finish, keys, values)
     else:
         buffers = arrived[0]
         per = keys.shape[1] // 64
-
-        def some(i, _):
+        for kept, old in zip(state, given):
+            kept[...] = old[...]
+
+        def some_pages(i, _):
             part = [buffers.at[i * per + k] for k in range(per)]
-            add_pages(slots, group, part, scaled_ref, state, keys, values)
+            add_pages(slots, group, part, scaled_ref, state, None, keys, values)
             return 0
 
-        lax.fori_loop(0, buffers.shape[0] // per, some, 0)
-    for h in range(kv_heads):
-        mixed[:, h] = (mixes[h] / sums[h]).reshape(count, group, width)
-    staged[...] = mixed[...].reshape(staged.shape).astype(BF16)
-    tail_count = out_ref.shape[1] - count
-    copy = pltpu.make_async_copy(staged, out_ref.at[0, pl.ds(tail_count, count)], sem)
-    copy.start()
-    copy.wait()
+        lax.fori_loop(0, buffers.shape[0] // per, some_pages, 0)
+        for h in range(kv_heads):
+            finish(h, sums[h], mixes[h])
+    for copy in copies:
+        copy.wait()
 
 
 def page_attention(scaled, state, out, arrived, slots):
@@ -404,9 +509,9 @@
         + [
             pltpu.VMEM((kv_heads, chunk, width), BF16),
             pltpu.VMEM((kv_heads, chunk, width), BF16),
-            pltpu.VMEM((count, kv_heads, group, width), F32),
+            pltpu.VMEM((kv_heads, count, group, width), F32),
             pltpu.VMEM((count, heads, width), BF16),
-            pltpu.SemaphoreType.DMA,
+            pltpu.SemaphoreType.DMA((kv_heads // 2,)),
         ],
         compiler_params=pltpu.CompilerParams(vmem_limit_bytes=48 * MIB),
         name="decode_pages",
@@ -436,28 +541,36 @@
 
     pages = page_rows.reshape(requests, page_depth * 2 * kv_heads, width)
     packed = pack(split, members, me.reshape(1), request_dest, request_slot, page_len, pages)
-    if split:
-        half = members // 2
-        swap = lambda block, k: lax.ppermute(block, "inst", [(i, i ^ k) for i in range(members)])
-        near = [packed[0]] + [swap(packed[k], k) for k in range(1, half)]
-        arrived = []
-        for k in range(members - 1, half - 1, -1):
-            arrived.append(swap(packed[k], k))
-    else:
-        near = []
-        arrived = [lax.all_to_all(packed[0], "inst", split_axis=0, concat_axis=0, tiled=True)]
-
-    out, scaled, *state = tail_attention(
+    keys, values_t, scaled, *state = sort_keys(
         prefix_len,
         cached_len,
         queries,
         kv_cache.reshape(-1, width),
         fresh_kv.reshape(-1, width),
         decode_cache.reshape(-1, width),
-        near,
         tail_count,
         kv_heads,
     )
+    if split:
+        half = members // 2
+        swap = lambda block, k: lax.ppermute(block, "inst", [(i, i ^ k) for i in range(members)])
+        arrived = list(packed)
+        for k in [*range(members - 1, members - 3, -1), *range(1, half)]:
+            arrived[k] = swap(packed[k], k)
+        later = range(half, members - 2)
+        keys, arrived[-1], *blocks = lax.optimization_barrier(
+            (keys, arrived[-1], *(packed[k] for k in later))
+        )
+        for k, block in zip(later, blocks):
+            arrived[k] = swap(block, k)
+    else:
+        arrived = [lax.all_to_all(packed[0], "inst", split_axis=0, concat_axis=0, tiled=True)]
+    out = tail_attention(prefix_len, queries, keys, values_t, tail_count)
+    if split:
+        out, *state = lax.optimization_barrier((out, *state))
+        first = arrived[:half] + arrived[: half + 1 : -1]
+        state = middle_pages(scaled, state, first, slots, heads // kv_heads)
+        arrived = arrived[half + 1 : half - 1 : -1]
     return page_attention(scaled, state, out, arrived, slots)
 
 

time: 48.4 us -> 47.3 us (0.977)
  the two profiles are of different devices: /device:TPU:28 before, /device:TPU:0 now
where the time goes in v3:
time: 47.3 us; the launch traced here: 47.1 us
  Pallas kernels  33.5 us (71%)
  starting transfers between devices  12.6 us (27%)
  between operations  0.92 us (2%)
    pallas_call x1, Pallas kernels, tail_attention(): pl.pallas_call(functools.partial(tail_kernel, scale, total - tail_count),...  25.5 us
    ppermute x7, starting transfers between devices, body(): lax.ppermute(block, 'inst', [(i, i ^ k) for i in range(members)])  12.6 us
    pallas_call x1, Pallas kernels, sort_keys(): pl.pallas_call(functools.partial(sort_kernel, scale, cached.shape[1]), ou...  2.99 us
    pallas_call x1, Pallas kernels, middle_pages(): pl.pallas_call(functools.partial(middle_kernel, slots, group), out_shape=...  1.92 us
    pallas_call x1, Pallas kernels, page_attention(): pl.pallas_call(functools.partial(page_kernel, slots), out_shape=jax.Shape...  1.75 us
    pallas_call x1, Pallas kernels, pack(): pl.pallas_call(functools.partial(pack_kernel, split), out_shape=out_shape...  1.33 us
  transfers between devices with their start and end apart: 7, of which 0 were waited for; matrix products, arithmetic and copies ran while one was open for 0% of the time, Pallas kernels for 65%

profile of v3, /device:TPU:0, one launch (start us, length us, event | category | flops | bytes accessed | tf_op | source)
XLA Modules:
  0.0 47.1 jit_solution(15506017554914646063)
XLA Ops:
  0.0 1.3 %pack_pages.1 = (bf16[528,128]{1,0:T(8,128)(2,1)S(1)}, bf16[528,128]{1,0:T(8,128)(2,1)S(1)}, bf16[528,128]{1,0:T(8,128)(2,1)S(1)}, bf16[528,128]{1,0:T(8,128)(2,...) custom-call(s32[1]{0:T(128)} %bitcast.3.me_ref, ...), custom_call_target="tpu_custom_call" | custom-call | tf_op jit(solution)/shard_map/pack_pages/pallas_call | solution.py:121
  1.3 6.1 %collective-permute-start = (bf16[528,128]{1,0:T(8,128)(2,1)S(1)}, bf16[528,128]{1,0:T(8,128)(2,1)S(1)}, u32[]{:S(2)}, u32[]{:S(2)}) collective-permute-start(bf16[528,128]{1,0:T(8,128)(2,1)S(1)} %get-tuple-element.32), channel_id=1, source_target_pairs={{0,14},{2,12},{4,10},{6,8},{8,6},{10,4},{12,2},{14,0},{1,15},{3,13... | collective-permute-start | bytes 405512 | tf_op jit(solution)/shard_map/ppermute | solution.py:556
  7.4 0.5 %collective-permute-start.1 = (bf16[528,128]{1,0:T(8,128)(2,1)S(1)}, bf16[528,128]{1,0:T(8,128)(2,1)S(1)}, u32[]{:S(2)}, u32[]{:S(2)}) collective-permute-start(bf16[528,128]{1,0:T(8,128)(2,1)S(1)} %get-tuple-element.44), channel_id=1, source_target_pairs={{0,2},{2,0},{4,6},{6,4},{8,10},{10,8},{12,14},{14,12},{1,3},{3,1},... | collective-permute-start | bytes 405512 | tf_op jit(solution)/shard_map/ppermute | solution.py:556
  7.9 0.0 collective-permute-start.2
  7.9 3.0 %collective-permute-start.3 = (bf16[528,128]{1,0:T(8,128)(2,1)S(1)}, bf16[528,128]{1,0:T(8,128)(2,1)S(1)}, u32[]{:S(2)}, u32[]{:S(2)}) collective-permute-start(bf16[528,128]{1,0:T(8,128)(2,1)S(1)} %get-tuple-element.46), channel_id=1, source_target_pairs={{0,6},{2,4},{4,2},{6,0},{8,14},{10,12},{12,10},{14,8},{1,7},{3,5},... | collective-permute-start | bytes 405512 | tf_op jit(solution)/shard_map/ppermute | solution.py:556
  10.9 0.2 collective-permute-start.4
  11.8 0.0 copy-start
  11.8 3.0 %sort_keys.1 = (bf16[4,1280,128]{2,1,0:T(8,128)(2,1)S(1)}, bf16[4,144,1280]{2,1,0:T(8,128)(2,1)S(1)}, bf16[4,128,256]{2,1,0:T(8,128)(2,1)S(1)}, f32[4,128,128]{2...) custom-call(s32[1]{0:T(128)S(6)} %copy.13.prefix_ref, s32[1,8]{1,0:T(1,128)} %cached_hbm.1, ...), custom_call_target="tpu_custom_call" | custom-call | flops 1 | bytes 12582912 | tf_op jit(solution)/shard_map/sort_keys/pallas_call | solution.py:260
  14.8 0.0 collective-permute-done.refs_4_
  14.8 1.6 %collective-permute-start.5 = (bf16[528,128]{1,0:T(8,128)(2,1)S(1)}, bf16[528,128]{1,0:T(8,128)(2,1)S(1)}, u32[]{:S(2)}, u32[]{:S(2)}) collective-permute-start(bf16[528,128]{1,0:T(8,128)(2,1)S(1)} %get-tuple-element.53), channel_id=1, source_target_pairs={{0,10},{2,8},{4,14},{6,12},{8,2},{10,0},{12,6},{14,4},{1,11},{3,9}... | collective-permute-start | bytes 405512 | tf_op jit(solution)/shard_map/ppermute | solution.py:556
  16.4 0.0 collective-permute-done.1.refs_1_
  16.4 1.2 %collective-permute-start.6 = (bf16[528,128]{1,0:T(8,128)(2,1)S(1)}, bf16[528,128]{1,0:T(8,128)(2,1)S(1)}, u32[]{:S(2)}, u32[]{:S(2)}) collective-permute-start(bf16[528,128]{1,0:T(8,128)(2,1)S(1)} %get-tuple-element.54), channel_id=1, source_target_pairs={{0,8},{2,10},{4,12},{6,14},{8,0},{10,2},{12,4},{14,6},{1,9},{3,11}... | collective-permute-start | bytes 405512 | tf_op jit(solution)/shard_map/ppermute | solution.py:556
  17.7 0.0 copy-done
  17.7 25.5 %tail_attention.1.out_in = bf16[1,272,32,128]{3,2,1,0:T(8,128)(2,1)} custom-call(s32[1]{0:T(128)S(6)} %copy.13.prefix_ref, bf16[1,272,32,128]{3,2,1,0:T(8,128)(2,1)S(1)} %copy-done, bf16[4,1280,128]{2,1,0:T(8,128)(2,1)S(1)} %get-tuple-element.35.keys, bf16[4,144,1280]{2,1,0:T(8,128)(2,1)S(1)} %get-tuple-element.36.values_t), custom_call_target="tpu_custom_call" | custom-call | flops 21474836480 | bytes 8388608 | tf_op jit(solution)/shard_map/tail_attention/pallas_call | solution.py:319
  43.2 0.0 collective-permute-done.2.refs_2_
  43.2 0.0 collective-permute-done.3.refs_3_
  43.2 0.0 collective-permute-done.4.refs_5_
  43.2 1.9 %middle_pages.1 = (f32[4,128,128]{2,1,0:T(8,128)S(1)}, f32[4,128,128]{2,1,0:T(8,128)S(1)}, f32[4,128,128]{2,1,0:T(8,128)S(1)}) custom-call(bf16[4,128,256]{2,1,0:T(8,128)(2,1)S(1)} %get-tuple-element.30.scaled_ref, f32[4,128,128]{2,1,0:T(8,128)S(1)} %get-tuple-element.40.m_in, f32[4,128,128]{2,1,0:T(8,128)S(1)} %get-tuple-element.41.l_in, ...), custom_call_target="tpu_custom_call" | custom-call | tf_op jit(solution)/shard_map/middle_pages/pallas_call | solution.py:442
  45.1 0.0 collective-permute-done.5.refs_0_
  45.2 0.0 collective-permute-done.6.refs_1_
  45.2 1.7 %decode_pages.1 = bf16[1,272,32,128]{3,2,1,0:T(8,128)(2,1)} custom-call(bf16[4,128,256]{2,1,0:T(8,128)(2,1)S(1)} %get-tuple-element.30.scaled_ref, f32[4,128,128]{2,1,0:T(8,128)S(1)} %get-tuple-element.49.m_in, f32[4,128,128]{2,1,0:T(8,128)S(1)} %get-tuple-element.50.l_in, ...), custom_call_target="tpu_custom_call", output_to_operand_aliasing={{}: (4, {})} | custom-call | tf_op jit(solution)/shard_map/decode_pages/pallas_call | solution.py:502
Async XLA Ops:
  1.3 13.4 %collective-permute-start = (bf16[528,128]{1,0:T(8,128)(2,1)S(1)}, bf16[528,128]{1,0:T(8,128)(2,1)S(1)}, u32[]{:S(2)}, u32[]{:S(2)}) collective-permute-start(bf16[528,128]{1,0:T(8,128)(2,1)S(1)} %get-tuple-element.32), channel_id=1, source_target_pairs={{0,14},{2,12},{4,10},{6,8},{8,6},{10,4},{12,2},{14,0},{1,15},{3,13... | collective-permute-start | bytes 405512 | tf_op jit(solution)/shard_map/ppermute | solution.py:556
  7.4 9.0 %collective-permute-start.1 = (bf16[528,128]{1,0:T(8,128)(2,1)S(1)}, bf16[528,128]{1,0:T(8,128)(2,1)S(1)}, u32[]{:S(2)}, u32[]{:S(2)}) collective-permute-start(bf16[528,128]{1,0:T(8,128)(2,1)S(1)} %get-tuple-element.44), channel_id=1, source_target_pairs={{0,2},{2,0},{4,6},{6,4},{8,10},{10,8},{12,14},{14,12},{1,3},{3,1},... | collective-permute-start | bytes 405512 | tf_op jit(solution)/shard_map/ppermute | solution.py:556
  7.9 35.3 %collective-permute-start.2 = (bf16[528,128]{1,0:T(8,128)(2,1)S(1)}, bf16[528,128]{1,0:T(8,128)(2,1)S(1)}, u32[]{:S(2)}, u32[]{:S(2)}) collective-permute-start(bf16[528,128]{1,0:T(8,128)(2,1)S(1)} %get-tuple-element.45), channel_id=1, source_target_pairs={{0,4},{2,6},{4,0},{6,2},{8,12},{10,14},{12,8},{14,10},{1,5},{3,7},... | collective-permute-start | bytes 405512 | tf_op jit(solution)/shard_map/ppermute | solution.py:556
  7.9 35.3 %collective-permute-start.3 = (bf16[528,128]{1,0:T(8,128)(2,1)S(1)}, bf16[528,128]{1,0:T(8,128)(2,1)S(1)}, u32[]{:S(2)}, u32[]{:S(2)}) collective-permute-start(bf16[528,128]{1,0:T(8,128)(2,1)S(1)} %get-tuple-element.46), channel_id=1, source_target_pairs={{0,6},{2,4},{4,2},{6,0},{8,14},{10,12},{12,10},{14,8},{1,7},{3,5},... | collective-permute-start | bytes 405512 | tf_op jit(solution)/shard_map/ppermute | solution.py:556
  10.9 32.3 %collective-permute-start.4 = (bf16[528,128]{1,0:T(8,128)(2,1)S(1)}, bf16[528,128]{1,0:T(8,128)(2,1)S(1)}, u32[]{:S(2)}, u32[]{:S(2)}) collective-permute-start(bf16[528,128]{1,0:T(8,128)(2,1)S(1)} %get-tuple-element.48), channel_id=1, source_target_pairs={{0,12},{2,14},{4,8},{6,10},{8,4},{10,6},{12,0},{14,2},{1,13},{3,15... | collective-permute-start | bytes 405512 | tf_op jit(solution)/shard_map/ppermute | solution.py:556
  11.8 5.9 %copy-start = (bf16[1,272,32,128]{3,2,1,0:T(8,128)(2,1)S(1)}, bf16[1,272,32,128]{3,2,1,0:T(8,128)(2,1)}, u32[]{:S(2)}) copy-start(bf16[1,272,32,128]{3,2,1,0:T(8,128)(2,1)} %q_ref.1) | copy-start | bytes 6684676
  14.8 30.4 %collective-permute-start.5 = (bf16[528,128]{1,0:T(8,128)(2,1)S(1)}, bf16[528,128]{1,0:T(8,128)(2,1)S(1)}, u32[]{:S(2)}, u32[]{:S(2)}) collective-permute-start(bf16[528,128]{1,0:T(8,128)(2,1)S(1)} %get-tuple-element.53), channel_id=1, source_target_pairs={{0,10},{2,8},{4,14},{6,12},{8,2},{10,0},{12,6},{14,4},{1,11},{3,9}... | collective-permute-start | bytes 405512 | tf_op jit(solution)/shard_map/ppermute | solution.py:556
  16.4 28.7 %collective-permute-start.6 = (bf16[528,128]{1,0:T(8,128)(2,1)S(1)}, bf16[528,128]{1,0:T(8,128)(2,1)S(1)}, u32[]{:S(2)}, u32[]{:S(2)}) collective-permute-start(bf16[528,128]{1,0:T(8,128)(2,1)S(1)} %get-tuple-element.54), channel_id=1, source_target_pairs={{0,8},{2,10},{4,12},{6,14},{8,0},{10,2},{12,4},{14,6},{1,9},{3,11}... | collective-permute-start | bytes 405512 | tf_op jit(solution)/shard_map/ppermute | solution.py:556

commit v4 on v3

--- a/solution.py
+++ b/solution.py
@@ -14,6 +14,7 @@
 BF16 = jnp.bfloat16
 META = 16
 MIB = 1 << 20
+FAR_ORDER = (0, 2, 1, 3)
 LOW, HIGH = 2.0**-40, 2.0**120
 
 
@@ -553,13 +554,14 @@
     )
     if split:
         half = members // 2
+        far = [half + i for i in FAR_ORDER] if half == len(FAR_ORDER) else list(range(half, members))
         swap = lambda block, k: lax.ppermute(block, "inst", [(i, i ^ k) for i in range(members)])
         arrived = list(packed)
-        for k in [*range(members - 1, members - 3, -1), *range(1, half)]:
+        for k in [*far[: half - 2], *range(1, half)]:
             arrived[k] = swap(packed[k], k)
-        later = range(half, members - 2)
-        keys, arrived[-1], *blocks = lax.optimization_barrier(
-            (keys, arrived[-1], *(packed[k] for k in later))
+        later = far[half - 2 :]
+        keys, arrived[far[0]], *blocks = lax.optimization_barrier(
+            (keys, arrived[far[0]], *(packed[k] for k in later))
         )
         for k, block in zip(later, blocks):
             arrived[k] = swap(block, k)
@@ -568,9 +570,9 @@
     out = tail_attention(prefix_len, queries, keys, values_t, tail_count)
     if split:
         out, *state = lax.optimization_barrier((out, *state))
-        first = arrived[:half] + arrived[: half + 1 : -1]
+        first = arrived[:half] + [arrived[k] for k in far[: half - 2]]
         state = middle_pages(scaled, state, first, slots, heads // kv_heads)
-        arrived = arrived[half + 1 : half - 1 : -1]
+        arrived = [arrived[k] for k in later]
     return page_attention(scaled, state, out, arrived, slots)
 
 

time: 47.3 us -> 47.1 us (level)
  no operation moved by 1% of the time
where the time goes in v4:
time: 47.1 us; the launch traced here: 47 us
  Pallas kernels  33.5 us (71%)
  starting transfers between devices  12.5 us (27%)
  between operations  0.92 us (2%)
    pallas_call x1, Pallas kernels, tail_attention(): pl.pallas_call(functools.partial(tail_kernel, scale, total - tail_count),...  25.5 us
    ppermute x7, starting transfers between devices, body(): lax.ppermute(block, 'inst', [(i, i ^ k) for i in range(members)])  12.5 us
    pallas_call x1, Pallas kernels, sort_keys(): pl.pallas_call(functools.partial(sort_kernel, scale, cached.shape[1]), ou...  3 us
    pallas_call x1, Pallas kernels, middle_pages(): pl.pallas_call(functools.partial(middle_kernel, slots, group), out_shape=...  1.92 us
    pallas_call x1, Pallas kernels, page_attention(): pl.pallas_call(functools.partial(page_kernel, slots), out_shape=jax.Shape...  1.75 us
    pallas_call x1, Pallas kernels, pack(): pl.pallas_call(functools.partial(pack_kernel, split), out_shape=out_shape...  1.33 us
  transfers between devices with their start and end apart: 7, of which 0 were waited for; matrix products, arithmetic and copies ran while one was open for 0% of the time, Pallas kernels for 65%

profile of v4, /device:TPU:0, one launch (start us, length us, event | category | flops | bytes accessed | tf_op | source)
XLA Modules:
  0.0 47.0 jit_solution(17454908098304971193)
XLA Ops:
  0.0 1.3 %pack_pages.1 = (bf16[528,128]{1,0:T(8,128)(2,1)S(1)}, bf16[528,128]{1,0:T(8,128)(2,1)S(1)}, bf16[528,128]{1,0:T(8,128)(2,1)S(1)}, bf16[528,128]{1,0:T(8,128)(2,...) custom-call(s32[1]{0:T(128)} %bitcast.3.me_ref, ...), custom_call_target="tpu_custom_call" | custom-call | tf_op jit(solution)/shard_map/pack_pages/pallas_call | solution.py:122
  1.3 4.1 %collective-permute-start = (bf16[528,128]{1,0:T(8,128)(2,1)S(1)}, bf16[528,128]{1,0:T(8,128)(2,1)S(1)}, u32[]{:S(2)}, u32[]{:S(2)}) collective-permute-start(bf16[528,128]{1,0:T(8,128)(2,1)S(1)} %get-tuple-element.32), channel_id=1, source_target_pairs={{0,8},{2,10},{4,12},{6,14},{8,0},{10,2},{12,4},{14,6},{1,9},{3,11}... | collective-permute-start | bytes 405512 | tf_op jit(solution)/shard_map/ppermute | solution.py:558
  5.4 1.5 %collective-permute-start.1 = (bf16[528,128]{1,0:T(8,128)(2,1)S(1)}, bf16[528,128]{1,0:T(8,128)(2,1)S(1)}, u32[]{:S(2)}, u32[]{:S(2)}) collective-permute-start(bf16[528,128]{1,0:T(8,128)(2,1)S(1)} %get-tuple-element.44), channel_id=1, source_target_pairs={{0,2},{2,0},{4,6},{6,4},{8,10},{10,8},{12,14},{14,12},{1,3},{3,1},... | collective-permute-start | bytes 405512 | tf_op jit(solution)/shard_map/ppermute | solution.py:558
  7.0 1.6 %collective-permute-start.2 = (bf16[528,128]{1,0:T(8,128)(2,1)S(1)}, bf16[528,128]{1,0:T(8,128)(2,1)S(1)}, u32[]{:S(2)}, u32[]{:S(2)}) collective-permute-start(bf16[528,128]{1,0:T(8,128)(2,1)S(1)} %get-tuple-element.45), channel_id=1, source_target_pairs={{0,4},{2,6},{4,0},{6,2},{8,12},{10,14},{12,8},{14,10},{1,5},{3,7},... | collective-permute-start | bytes 405512 | tf_op jit(solution)/shard_map/ppermute | solution.py:558
  8.5 0.4 collective-permute-start.3
  8.9 1.3 %collective-permute-start.4 = (bf16[528,128]{1,0:T(8,128)(2,1)S(1)}, bf16[528,128]{1,0:T(8,128)(2,1)S(1)}, u32[]{:S(2)}, u32[]{:S(2)}) collective-permute-start(bf16[528,128]{1,0:T(8,128)(2,1)S(1)} %get-tuple-element.48), channel_id=1, source_target_pairs={{0,12},{2,14},{4,8},{6,10},{8,4},{10,6},{12,0},{14,2},{1,13},{3,15... | collective-permute-start | bytes 405512 | tf_op jit(solution)/shard_map/ppermute | solution.py:558
  10.9 0.0 copy-start
  10.9 3.0 %sort_keys.1 = (bf16[4,1280,128]{2,1,0:T(8,128)(2,1)S(1)}, bf16[4,144,1280]{2,1,0:T(8,128)(2,1)S(1)}, bf16[4,128,256]{2,1,0:T(8,128)(2,1)S(1)}, f32[4,128,128]{2...) custom-call(s32[1]{0:T(128)S(6)} %copy.13.prefix_ref, s32[1,8]{1,0:T(1,128)} %cached_hbm.1, ...), custom_call_target="tpu_custom_call" | custom-call | flops 1 | bytes 12582912 | tf_op jit(solution)/shard_map/sort_keys/pallas_call | solution.py:261
  14.0 0.0 collective-permute-done.refs_4_
  14.0 2.7 %collective-permute-start.5 = (bf16[528,128]{1,0:T(8,128)(2,1)S(1)}, bf16[528,128]{1,0:T(8,128)(2,1)S(1)}, u32[]{:S(2)}, u32[]{:S(2)}) collective-permute-start(bf16[528,128]{1,0:T(8,128)(2,1)S(1)} %get-tuple-element.53), channel_id=1, source_target_pairs={{0,10},{2,8},{4,14},{6,12},{8,2},{10,0},{12,6},{14,4},{1,11},{3,9}... | collective-permute-start | bytes 405512 | tf_op jit(solution)/shard_map/ppermute | solution.py:558
  16.7 0.0 collective-permute-done.1.refs_1_
  16.7 0.9 %collective-permute-start.6 = (bf16[528,128]{1,0:T(8,128)(2,1)S(1)}, bf16[528,128]{1,0:T(8,128)(2,1)S(1)}, u32[]{:S(2)}, u32[]{:S(2)}) collective-permute-start(bf16[528,128]{1,0:T(8,128)(2,1)S(1)} %get-tuple-element.54), channel_id=1, source_target_pairs={{0,14},{2,12},{4,10},{6,8},{8,6},{10,4},{12,2},{14,0},{1,15},{3,13... | collective-permute-start | bytes 405512 | tf_op jit(solution)/shard_map/ppermute | solution.py:558
  17.5 0.0 copy-done
  17.5 25.5 %tail_attention.1.out_in = bf16[1,272,32,128]{3,2,1,0:T(8,128)(2,1)} custom-call(s32[1]{0:T(128)S(6)} %copy.13.prefix_ref, bf16[1,272,32,128]{3,2,1,0:T(8,128)(2,1)S(1)} %copy-done, bf16[4,1280,128]{2,1,0:T(8,128)(2,1)S(1)} %get-tuple-element.35.keys, bf16[4,144,1280]{2,1,0:T(8,128)(2,1)S(1)} %get-tuple-element.36.values_t), custom_call_target="tpu_custom_call" | custom-call | flops 21474836480 | bytes 8388608 | tf_op jit(solution)/shard_map/tail_attention/pallas_call | solution.py:320
  43.1 0.0 collective-permute-done.2.refs_2_
  43.1 0.0 collective-permute-done.3.refs_3_
  43.1 0.0 collective-permute-done.4.refs_5_
  43.1 1.9 %middle_pages.1 = (f32[4,128,128]{2,1,0:T(8,128)S(1)}, f32[4,128,128]{2,1,0:T(8,128)S(1)}, f32[4,128,128]{2,1,0:T(8,128)S(1)}) custom-call(bf16[4,128,256]{2,1,0:T(8,128)(2,1)S(1)} %get-tuple-element.30.scaled_ref, f32[4,128,128]{2,1,0:T(8,128)S(1)} %get-tuple-element.40.m_in, f32[4,128,128]{2,1,0:T(8,128)S(1)} %get-tuple-element.41.l_in, ...), custom_call_target="tpu_custom_call" | custom-call | tf_op jit(solution)/shard_map/middle_pages/pallas_call | solution.py:443
  45.0 0.0 collective-permute-done.5.refs_0_
  45.0 0.0 collective-permute-done.6.refs_1_
  45.1 1.7 %decode_pages.1 = bf16[1,272,32,128]{3,2,1,0:T(8,128)(2,1)} custom-call(bf16[4,128,256]{2,1,0:T(8,128)(2,1)S(1)} %get-tuple-element.30.scaled_ref, f32[4,128,128]{2,1,0:T(8,128)S(1)} %get-tuple-element.49.m_in, f32[4,128,128]{2,1,0:T(8,128)S(1)} %get-tuple-element.50.l_in, ...), custom_call_target="tpu_custom_call", output_to_operand_aliasing={{}: (4, {})} | custom-call | tf_op jit(solution)/shard_map/decode_pages/pallas_call | solution.py:503
Async XLA Ops:
  1.3 12.6 %collective-permute-start = (bf16[528,128]{1,0:T(8,128)(2,1)S(1)}, bf16[528,128]{1,0:T(8,128)(2,1)S(1)}, u32[]{:S(2)}, u32[]{:S(2)}) collective-permute-start(bf16[528,128]{1,0:T(8,128)(2,1)S(1)} %get-tuple-element.32), channel_id=1, source_target_pairs={{0,8},{2,10},{4,12},{6,14},{8,0},{10,2},{12,4},{14,6},{1,9},{3,11}... | collective-permute-start | bytes 405512 | tf_op jit(solution)/shard_map/ppermute | solution.py:558
  5.4 11.2 %collective-permute-start.1 = (bf16[528,128]{1,0:T(8,128)(2,1)S(1)}, bf16[528,128]{1,0:T(8,128)(2,1)S(1)}, u32[]{:S(2)}, u32[]{:S(2)}) collective-permute-start(bf16[528,128]{1,0:T(8,128)(2,1)S(1)} %get-tuple-element.44), channel_id=1, source_target_pairs={{0,2},{2,0},{4,6},{6,4},{8,10},{10,8},{12,14},{14,12},{1,3},{3,1},... | collective-permute-start | bytes 405512 | tf_op jit(solution)/shard_map/ppermute | solution.py:558
  7.0 36.1 %collective-permute-start.2 = (bf16[528,128]{1,0:T(8,128)(2,1)S(1)}, bf16[528,128]{1,0:T(8,128)(2,1)S(1)}, u32[]{:S(2)}, u32[]{:S(2)}) collective-permute-start(bf16[528,128]{1,0:T(8,128)(2,1)S(1)} %get-tuple-element.45), channel_id=1, source_target_pairs={{0,4},{2,6},{4,0},{6,2},{8,12},{10,14},{12,8},{14,10},{1,5},{3,7},... | collective-permute-start | bytes 405512 | tf_op jit(solution)/shard_map/ppermute | solution.py:558
  8.5 34.6 %collective-permute-start.3 = (bf16[528,128]{1,0:T(8,128)(2,1)S(1)}, bf16[528,128]{1,0:T(8,128)(2,1)S(1)}, u32[]{:S(2)}, u32[]{:S(2)}) collective-permute-start(bf16[528,128]{1,0:T(8,128)(2,1)S(1)} %get-tuple-element.46), channel_id=1, source_target_pairs={{0,6},{2,4},{4,2},{6,0},{8,14},{10,12},{12,10},{14,8},{1,7},{3,5},... | collective-permute-start | bytes 405512 | tf_op jit(solution)/shard_map/ppermute | solution.py:558
  8.9 34.2 %collective-permute-start.4 = (bf16[528,128]{1,0:T(8,128)(2,1)S(1)}, bf16[528,128]{1,0:T(8,128)(2,1)S(1)}, u32[]{:S(2)}, u32[]{:S(2)}) collective-permute-start(bf16[528,128]{1,0:T(8,128)(2,1)S(1)} %get-tuple-element.48), channel_id=1, source_target_pairs={{0,12},{2,14},{4,8},{6,10},{8,4},{10,6},{12,0},{14,2},{1,13},{3,15... | collective-permute-start | bytes 405512 | tf_op jit(solution)/shard_map/ppermute | solution.py:558
  10.9 6.6 %copy-start = (bf16[1,272,32,128]{3,2,1,0:T(8,128)(2,1)S(1)}, bf16[1,272,32,128]{3,2,1,0:T(8,128)(2,1)}, u32[]{:S(2)}) copy-start(bf16[1,272,32,128]{3,2,1,0:T(8,128)(2,1)} %q_ref.1) | copy-start | bytes 6684676
  14.0 31.1 %collective-permute-start.5 = (bf16[528,128]{1,0:T(8,128)(2,1)S(1)}, bf16[528,128]{1,0:T(8,128)(2,1)S(1)}, u32[]{:S(2)}, u32[]{:S(2)}) collective-permute-start(bf16[528,128]{1,0:T(8,128)(2,1)S(1)} %get-tuple-element.53), channel_id=1, source_target_pairs={{0,10},{2,8},{4,14},{6,12},{8,2},{10,0},{12,6},{14,4},{1,11},{3,9}... | collective-permute-start | bytes 405512 | tf_op jit(solution)/shard_map/ppermute | solution.py:558
  16.7 28.4 %collective-permute-start.6 = (bf16[528,128]{1,0:T(8,128)(2,1)S(1)}, bf16[528,128]{1,0:T(8,128)(2,1)S(1)}, u32[]{:S(2)}, u32[]{:S(2)}) collective-permute-start(bf16[528,128]{1,0:T(8,128)(2,1)S(1)} %get-tuple-element.54), channel_id=1, source_target_pairs={{0,14},{2,12},{4,10},{6,8},{8,6},{10,4},{12,2},{14,0},{1,15},{3,13... | collective-permute-start | bytes 405512 | tf_op jit(solution)/shard_map/ppermute | solution.py:558

commit v5 on v4

--- a/solution.py
+++ b/solution.py
@@ -14,7 +14,7 @@
 BF16 = jnp.bfloat16
 META = 16
 MIB = 1 << 20
-FAR_ORDER = (0, 2, 1, 3)
+FAR_ORDER = (0, 3, 1, 2)
 LOW, HIGH = 2.0**-40, 2.0**120
 
 
@@ -392,7 +392,7 @@
         mixes[h] = summed[:, :width]
 
 
-def add_pages(slots, group, buffers, scaled_ref, state, finish, keys, values, target=None):
+def add_pages(slots, group, buffers, scaled_ref, state, finish, keys, values):
     kv_heads, rows, width = state[0].shape
     kinds = 2 * kv_heads
     page_rows = (buffers[0].shape[0] - META) // PAIR
@@ -427,28 +427,8 @@
         if finish:
             finish(h, weight_sum, mix)
         else:
-            for kept, new in zip(target or state, (peak, weight_sum, mix)):
+            for kept, new in zip(state, (peak, weight_sum, mix)):
                 kept[h] = new
-
-
-def middle_kernel(slots, group, scaled_ref, m_in, l_in, a_in, *refs):
-    *arrived, peaks, sums, mixes, keys, values = refs
-    given, state = (m_in, l_in, a_in), (peaks, sums, mixes)
-    add_pages(slots, group, arrived, scaled_ref, given, None, keys, values, state)
-
-
-def middle_pages(scaled, state, arrived, slots, group):
-    kv_heads, rows, width = state[0].shape
-    vmem = pl.BlockSpec(memory_space=pltpu.VMEM)
-    return pl.pallas_call(
-        functools.partial(middle_kernel, slots, group),
-        out_shape=[jax.ShapeDtypeStruct(state[0].shape, F32)] * 3,
-        in_specs=[vmem] * (4 + len(arrived)),
-        out_specs=[vmem] * 3,
-        scratch_shapes=[pltpu.VMEM((kv_heads, 64 * len(arrived), width), BF16)] * 2,
-        compiler_params=pltpu.CompilerParams(vmem_limit_bytes=16 * MIB),
-        name="middle_pages",
-    )(scaled, *state, *arrived)
 
 
 def page_kernel(slots, scaled_ref, m_in, l_in, a_in, out_in, *refs):
@@ -569,10 +549,7 @@
         arrived = [lax.all_to_all(packed[0], "inst", split_axis=0, concat_axis=0, tiled=True)]
     out = tail_attention(prefix_len, queries, keys, values_t, tail_count)
     if split:
-        out, *state = lax.optimization_barrier((out, *state))
-        first = arrived[:half] + [arrived[k] for k in far[: half - 2]]
-        state = middle_pages(scaled, state, first, slots, heads // kv_heads)
-        arrived = [arrived[k] for k in later]
+        arrived = arrived[:half] + [arrived[k] for k in far]
     return page_attention(scaled, state, out, arrived, slots)
 
 

time: 47.1 us -> 46.2 us (0.981)
  Pallas kernels: 33.5 us -> 32.6 us
    pallas_call x1 -> x0, Pallas kernels: 1.92 us -> none  [middle_pages(): pl.pallas_call(functools.partial(middle_kernel, slots, group), out_shape=...]
    pallas_call x1, Pallas kernels: 1.75 us -> 2.73 us  [page_attention(): pl.pallas_call(functools.partial(page_kernel, slots), out_shape=jax.Shape...]
  transfers between devices with their start and end apart: 7 -> 7, of which waited for: 0 -> 0; matrix products, arithmetic and copies ran while one was open for 0% -> 0% of each run, Pallas kernels for 65% -> 62%
where the time goes in v5:
time: 46.2 us; the launch traced here: 46.1 us
  Pallas kernels  32.6 us (71%)
  starting transfers between devices  12.6 us (27%)
  between operations  0.92 us (2%)
    pallas_call x1, Pallas kernels, tail_attention(): pl.pallas_call(functools.partial(tail_kernel, scale, total - tail_count),...  25.5 us
    ppermute x7, starting transfers between devices, body(): lax.ppermute(block, 'inst', [(i, i ^ k) for i in range(members)])  12.6 us
    pallas_call x1, Pallas kernels, sort_keys(): pl.pallas_call(functools.partial(sort_kernel, scale, cached.shape[1]), ou...  2.99 us
    pallas_call x1, Pallas kernels, page_attention(): pl.pallas_call(functools.partial(page_kernel, slots), out_shape=jax.Shape...  2.73 us
    pallas_call x1, Pallas kernels, pack(): pl.pallas_call(functools.partial(pack_kernel, split), out_shape=out_shape...  1.33 us
  transfers between devices with their start and end apart: 7, of which 0 were waited for; matrix products, arithmetic and copies ran while one was open for 0% of the time, Pallas kernels for 62%

profile of v5, /device:TPU:0, one launch (start us, length us, event | category | flops | bytes accessed | tf_op | source)
XLA Modules:
  0.0 46.1 jit_solution(5100270659417401192)
XLA Ops:
  0.0 1.3 %pack_pages.1 = (bf16[528,128]{1,0:T(8,128)(2,1)S(1)}, bf16[528,128]{1,0:T(8,128)(2,1)S(1)}, bf16[528,128]{1,0:T(8,128)(2,1)S(1)}, bf16[528,128]{1,0:T(8,128)(2,...) custom-call(s32[1]{0:T(128)} %bitcast.3.me_ref, ...), custom_call_target="tpu_custom_call" | custom-call | tf_op jit(solution)/shard_map/pack_pages/pallas_call | solution.py:122
  1.3 4.1 %collective-permute-start = (bf16[528,128]{1,0:T(8,128)(2,1)S(1)}, bf16[528,128]{1,0:T(8,128)(2,1)S(1)}, u32[]{:S(2)}, u32[]{:S(2)}) collective-permute-start(bf16[528,128]{1,0:T(8,128)(2,1)S(1)} %get-tuple-element.28), channel_id=1, source_target_pairs={{0,8},{2,10},{4,12},{6,14},{8,0},{10,2},{12,4},{14,6},{1,9},{3,11}... | collective-permute-start | bytes 405512 | tf_op jit(solution)/shard_map/ppermute | solution.py:538
  5.4 1.5 %collective-permute-start.1 = (bf16[528,128]{1,0:T(8,128)(2,1)S(1)}, bf16[528,128]{1,0:T(8,128)(2,1)S(1)}, u32[]{:S(2)}, u32[]{:S(2)}) collective-permute-start(bf16[528,128]{1,0:T(8,128)(2,1)S(1)} %get-tuple-element.34), channel_id=1, source_target_pairs={{0,2},{2,0},{4,6},{6,4},{8,10},{10,8},{12,14},{14,12},{1,3},{3,1},... | collective-permute-start | bytes 405512 | tf_op jit(solution)/shard_map/ppermute | solution.py:538
  7.0 1.6 %collective-permute-start.2 = (bf16[528,128]{1,0:T(8,128)(2,1)S(1)}, bf16[528,128]{1,0:T(8,128)(2,1)S(1)}, u32[]{:S(2)}, u32[]{:S(2)}) collective-permute-start(bf16[528,128]{1,0:T(8,128)(2,1)S(1)} %get-tuple-element.35), channel_id=1, source_target_pairs={{0,4},{2,6},{4,0},{6,2},{8,12},{10,14},{12,8},{14,10},{1,5},{3,7},... | collective-permute-start | bytes 405512 | tf_op jit(solution)/shard_map/ppermute | solution.py:538
  8.5 0.4 collective-permute-start.3
  8.9 2.3 %collective-permute-start.4 = (bf16[528,128]{1,0:T(8,128)(2,1)S(1)}, bf16[528,128]{1,0:T(8,128)(2,1)S(1)}, u32[]{:S(2)}, u32[]{:S(2)}) collective-permute-start(bf16[528,128]{1,0:T(8,128)(2,1)S(1)} %get-tuple-element.38), channel_id=1, source_target_pairs={{0,14},{2,12},{4,10},{6,8},{8,6},{10,4},{12,2},{14,0},{1,15},{3,13... | collective-permute-start | bytes 405512 | tf_op jit(solution)/shard_map/ppermute | solution.py:538
  11.9 0.0 copy-start
  11.9 3.0 %sort_keys.1 = (bf16[4,1280,128]{2,1,0:T(8,128)(2,1)S(1)}, bf16[4,144,1280]{2,1,0:T(8,128)(2,1)S(1)}, bf16[4,128,256]{2,1,0:T(8,128)(2,1)S(1)}, f32[4,128,128]{2...) custom-call(s32[1]{0:T(128)S(6)} %copy.13.prefix_ref, s32[1,8]{1,0:T(1,128)} %cached_hbm.1, ...), custom_call_target="tpu_custom_call" | custom-call | flops 1 | bytes 12582912 | tf_op jit(solution)/shard_map/sort_keys/pallas_call | solution.py:261
  14.9 0.0 collective-permute-done.refs_4_
  14.9 1.7 %collective-permute-start.5 = (bf16[528,128]{1,0:T(8,128)(2,1)S(1)}, bf16[528,128]{1,0:T(8,128)(2,1)S(1)}, u32[]{:S(2)}, u32[]{:S(2)}) collective-permute-start(bf16[528,128]{1,0:T(8,128)(2,1)S(1)} %get-tuple-element.39), channel_id=1, source_target_pairs={{0,10},{2,8},{4,14},{6,12},{8,2},{10,0},{12,6},{14,4},{1,11},{3,9}... | collective-permute-start | bytes 405512 | tf_op jit(solution)/shard_map/ppermute | solution.py:538
  16.6 0.0 collective-permute-done.1.refs_1_
  16.6 1.0 %collective-permute-start.6 = (bf16[528,128]{1,0:T(8,128)(2,1)S(1)}, bf16[528,128]{1,0:T(8,128)(2,1)S(1)}, u32[]{:S(2)}, u32[]{:S(2)}) collective-permute-start(bf16[528,128]{1,0:T(8,128)(2,1)S(1)} %get-tuple-element.40), channel_id=1, source_target_pairs={{0,12},{2,14},{4,8},{6,10},{8,4},{10,6},{12,0},{14,2},{1,13},{3,15... | collective-permute-start | bytes 405512 | tf_op jit(solution)/shard_map/ppermute | solution.py:538
  17.6 0.0 copy-done
  17.6 25.5 %tail_attention.1.out_in = bf16[1,272,32,128]{3,2,1,0:T(8,128)(2,1)} custom-call(s32[1]{0:T(128)S(6)} %copy.13.prefix_ref, bf16[1,272,32,128]{3,2,1,0:T(8,128)(2,1)S(1)} %copy-done, bf16[4,1280,128]{2,1,0:T(8,128)(2,1)S(1)} %get-tuple-element.31.keys, bf16[4,144,1280]{2,1,0:T(8,128)(2,1)S(1)} %get-tuple-element.32.values_t), custom_call_target="tpu_custom_call" | custom-call | flops 21474836480 | bytes 8388608 | tf_op jit(solution)/shard_map/tail_attention/pallas_call | solution.py:320
  43.1 0.0 collective-permute-done.2.refs_2_
  43.1 0.0 collective-permute-done.3.refs_3_
  43.1 0.0 collective-permute-done.4.refs_5_
  43.1 0.0 collective-permute-done.5.refs_6_
  43.2 0.0 collective-permute-done.6.refs_7_
  43.2 2.7 %decode_pages.1 = bf16[1,272,32,128]{3,2,1,0:T(8,128)(2,1)} custom-call(bf16[4,128,256]{2,1,0:T(8,128)(2,1)S(1)} %get-tuple-element.23.scaled_ref, f32[4,128,128]{2,1,0:T(8,128)S(1)} %get-tuple-element.24.m_in, f32[4,128,128]{2,1,0:T(8,128)S(1)} %get-tuple-element.25.l_in, ...), custom_call_target="tpu_custom_call", output_to_operand_aliasing={{}: (4, {})} | custom-call | tf_op jit(solution)/shard_map/decode_pages/pallas_call | solution.py:483
Async XLA Ops:
  1.3 13.6 %collective-permute-start = (bf16[528,128]{1,0:T(8,128)(2,1)S(1)}, bf16[528,128]{1,0:T(8,128)(2,1)S(1)}, u32[]{:S(2)}, u32[]{:S(2)}) collective-permute-start(bf16[528,128]{1,0:T(8,128)(2,1)S(1)} %get-tuple-element.28), channel_id=1, source_target_pairs={{0,8},{2,10},{4,12},{6,14},{8,0},{10,2},{12,4},{14,6},{1,9},{3,11}... | collective-permute-start | bytes 405512 | tf_op jit(solution)/shard_map/ppermute | solution.py:538
  5.4 11.2 %collective-permute-start.1 = (bf16[528,128]{1,0:T(8,128)(2,1)S(1)}, bf16[528,128]{1,0:T(8,128)(2,1)S(1)}, u32[]{:S(2)}, u32[]{:S(2)}) collective-permute-start(bf16[528,128]{1,0:T(8,128)(2,1)S(1)} %get-tuple-element.34), channel_id=1, source_target_pairs={{0,2},{2,0},{4,6},{6,4},{8,10},{10,8},{12,14},{14,12},{1,3},{3,1},... | collective-permute-start | bytes 405512 | tf_op jit(solution)/shard_map/ppermute | solution.py:538
  7.0 36.1 %collective-permute-start.2 = (bf16[528,128]{1,0:T(8,128)(2,1)S(1)}, bf16[528,128]{1,0:T(8,128)(2,1)S(1)}, u32[]{:S(2)}, u32[]{:S(2)}) collective-permute-start(bf16[528,128]{1,0:T(8,128)(2,1)S(1)} %get-tuple-element.35), channel_id=1, source_target_pairs={{0,4},{2,6},{4,0},{6,2},{8,12},{10,14},{12,8},{14,10},{1,5},{3,7},... | collective-permute-start | bytes 405512 | tf_op jit(solution)/shard_map/ppermute | solution.py:538
  8.5 34.6 %collective-permute-start.3 = (bf16[528,128]{1,0:T(8,128)(2,1)S(1)}, bf16[528,128]{1,0:T(8,128)(2,1)S(1)}, u32[]{:S(2)}, u32[]{:S(2)}) collective-permute-start(bf16[528,128]{1,0:T(8,128)(2,1)S(1)} %get-tuple-element.36), channel_id=1, source_target_pairs={{0,6},{2,4},{4,2},{6,0},{8,14},{10,12},{12,10},{14,8},{1,7},{3,5},... | collective-permute-start | bytes 405512 | tf_op jit(solution)/shard_map/ppermute | solution.py:538
  8.9 34.2 %collective-permute-start.4 = (bf16[528,128]{1,0:T(8,128)(2,1)S(1)}, bf16[528,128]{1,0:T(8,128)(2,1)S(1)}, u32[]{:S(2)}, u32[]{:S(2)}) collective-permute-start(bf16[528,128]{1,0:T(8,128)(2,1)S(1)} %get-tuple-element.38), channel_id=1, source_target_pairs={{0,14},{2,12},{4,10},{6,8},{8,6},{10,4},{12,2},{14,0},{1,15},{3,13... | collective-permute-start | bytes 405512 | tf_op jit(solution)/shard_map/ppermute | solution.py:538
  11.9 5.7 %copy-start = (bf16[1,272,32,128]{3,2,1,0:T(8,128)(2,1)S(1)}, bf16[1,272,32,128]{3,2,1,0:T(8,128)(2,1)}, u32[]{:S(2)}) copy-start(bf16[1,272,32,128]{3,2,1,0:T(8,128)(2,1)} %q_ref.1) | copy-start | bytes 6684676
  14.9 28.2 %collective-permute-start.5 = (bf16[528,128]{1,0:T(8,128)(2,1)S(1)}, bf16[528,128]{1,0:T(8,128)(2,1)S(1)}, u32[]{:S(2)}, u32[]{:S(2)}) collective-permute-start(bf16[528,128]{1,0:T(8,128)(2,1)S(1)} %get-tuple-element.39), channel_id=1, source_target_pairs={{0,10},{2,8},{4,14},{6,12},{8,2},{10,0},{12,6},{14,4},{1,11},{3,9}... | collective-permute-start | bytes 405512 | tf_op jit(solution)/shard_map/ppermute | solution.py:538
  16.6 26.5 %collective-permute-start.6 = (bf16[528,128]{1,0:T(8,128)(2,1)S(1)}, bf16[528,128]{1,0:T(8,128)(2,1)S(1)}, u32[]{:S(2)}, u32[]{:S(2)}) collective-permute-start(bf16[528,128]{1,0:T(8,128)(2,1)S(1)} %get-tuple-element.40), channel_id=1, source_target_pairs={{0,12},{2,14},{4,8},{6,10},{8,4},{10,6},{12,0},{14,2},{1,13},{3,15... | collective-permute-start | bytes 405512 | tf_op jit(solution)/shard_map/ppermute | solution.py:538

commit v6 on v5

--- a/solution.py
+++ b/solution.py
@@ -12,7 +12,7 @@
 NEG = -1e30
 F32 = jnp.float32
 BF16 = jnp.bfloat16
-META = 16
+META = 8
 MIB = 1 << 20
 FAR_ORDER = (0, 3, 1, 2)
 LOW, HIGH = 2.0**-40, 2.0**120

time: 46.2 us -> 46.2 us (level)
  no operation moved by 1% of the time
where the time goes in v6:
time: 46.2 us; the launch traced here: 46.1 us
  Pallas kernels  32.6 us (71%)
  starting transfers between devices  12.6 us (27%)
  between operations  0.92 us (2%)
    pallas_call x1, Pallas kernels, tail_attention(): pl.pallas_call(functools.partial(tail_kernel, scale, total - tail_count),...  25.5 us
    ppermute x7, starting transfers between devices, body(): lax.ppermute(block, 'inst', [(i, i ^ k) for i in range(members)])  12.6 us
    pallas_call x1, Pallas kernels, sort_keys(): pl.pallas_call(functools.partial(sort_kernel, scale, cached.shape[1]), ou...  2.99 us
    pallas_call x1, Pallas kernels, page_attention(): pl.pallas_call(functools.partial(page_kernel, slots), out_shape=jax.Shape...  2.73 us
    pallas_call x1, Pallas kernels, pack(): pl.pallas_call(functools.partial(pack_kernel, split), out_shape=out_shape...  1.33 us
  transfers between devices with their start and end apart: 7, of which 0 were waited for; matrix products, arithmetic and copies ran while one was open for 0% of the time, Pallas kernels for 62%

profile of v6, /device:TPU:0, one launch (start us, length us, event | category | flops | bytes accessed | tf_op | source)
XLA Modules:
  0.0 46.1 jit_solution(3917427611531739337)
XLA Ops:
  0.0 1.3 %pack_pages.1 = (bf16[520,128]{1,0:T(8,128)(2,1)S(1)}, bf16[520,128]{1,0:T(8,128)(2,1)S(1)}, bf16[520,128]{1,0:T(8,128)(2,1)S(1)}, bf16[520,128]{1,0:T(8,128)(2,...) custom-call(s32[1]{0:T(128)} %bitcast.3.me_ref, ...), custom_call_target="tpu_custom_call" | custom-call | tf_op jit(solution)/shard_map/pack_pages/pallas_call | solution.py:122
  1.3 4.1 %collective-permute-start = (bf16[520,128]{1,0:T(8,128)(2,1)S(1)}, bf16[520,128]{1,0:T(8,128)(2,1)S(1)}, u32[]{:S(2)}, u32[]{:S(2)}) collective-permute-start(bf16[520,128]{1,0:T(8,128)(2,1)S(1)} %get-tuple-element.28), channel_id=1, source_target_pairs={{0,8},{2,10},{4,12},{6,14},{8,0},{10,2},{12,4},{14,6},{1,9},{3,11}... | collective-permute-start | bytes 399368 | tf_op jit(solution)/shard_map/ppermute | solution.py:538
  5.4 1.5 %collective-permute-start.1 = (bf16[520,128]{1,0:T(8,128)(2,1)S(1)}, bf16[520,128]{1,0:T(8,128)(2,1)S(1)}, u32[]{:S(2)}, u32[]{:S(2)}) collective-permute-start(bf16[520,128]{1,0:T(8,128)(2,1)S(1)} %get-tuple-element.34), channel_id=1, source_target_pairs={{0,2},{2,0},{4,6},{6,4},{8,10},{10,8},{12,14},{14,12},{1,3},{3,1},... | collective-permute-start | bytes 399368 | tf_op jit(solution)/shard_map/ppermute | solution.py:538
  7.0 1.6 %collective-permute-start.2 = (bf16[520,128]{1,0:T(8,128)(2,1)S(1)}, bf16[520,128]{1,0:T(8,128)(2,1)S(1)}, u32[]{:S(2)}, u32[]{:S(2)}) collective-permute-start(bf16[520,128]{1,0:T(8,128)(2,1)S(1)} %get-tuple-element.35), channel_id=1, source_target_pairs={{0,4},{2,6},{4,0},{6,2},{8,12},{10,14},{12,8},{14,10},{1,5},{3,7},... | collective-permute-start | bytes 399368 | tf_op jit(solution)/shard_map/ppermute | solution.py:538
  8.5 0.4 collective-permute-start.3
  8.9 2.3 %collective-permute-start.4 = (bf16[520,128]{1,0:T(8,128)(2,1)S(1)}, bf16[520,128]{1,0:T(8,128)(2,1)S(1)}, u32[]{:S(2)}, u32[]{:S(2)}) collective-permute-start(bf16[520,128]{1,0:T(8,128)(2,1)S(1)} %get-tuple-element.38), channel_id=1, source_target_pairs={{0,14},{2,12},{4,10},{6,8},{8,6},{10,4},{12,2},{14,0},{1,15},{3,13... | collective-permute-start | bytes 399368 | tf_op jit(solution)/shard_map/ppermute | solution.py:538
  11.9 0.0 copy-start
  11.9 3.0 %sort_keys.1 = (bf16[4,1280,128]{2,1,0:T(8,128)(2,1)S(1)}, bf16[4,144,1280]{2,1,0:T(8,128)(2,1)S(1)}, bf16[4,128,256]{2,1,0:T(8,128)(2,1)S(1)}, f32[4,128,128]{2...) custom-call(s32[1]{0:T(128)S(6)} %copy.13.prefix_ref, s32[1,8]{1,0:T(1,128)} %cached_hbm.1, ...), custom_call_target="tpu_custom_call" | custom-call | flops 1 | bytes 12582912 | tf_op jit(solution)/shard_map/sort_keys/pallas_call | solution.py:261
  14.9 0.0 collective-permute-done.refs_4_
  14.9 1.7 %collective-permute-start.5 = (bf16[520,128]{1,0:T(8,128)(2,1)S(1)}, bf16[520,128]{1,0:T(8,128)(2,1)S(1)}, u32[]{:S(2)}, u32[]{:S(2)}) collective-permute-start(bf16[520,128]{1,0:T(8,128)(2,1)S(1)} %get-tuple-element.39), channel_id=1, source_target_pairs={{0,10},{2,8},{4,14},{6,12},{8,2},{10,0},{12,6},{14,4},{1,11},{3,9}... | collective-permute-start | bytes 399368 | tf_op jit(solution)/shard_map/ppermute | solution.py:538
  16.6 0.0 collective-permute-done.1.refs_1_
  16.6 1.0 %collective-permute-start.6 = (bf16[520,128]{1,0:T(8,128)(2,1)S(1)}, bf16[520,128]{1,0:T(8,128)(2,1)S(1)}, u32[]{:S(2)}, u32[]{:S(2)}) collective-permute-start(bf16[520,128]{1,0:T(8,128)(2,1)S(1)} %get-tuple-element.40), channel_id=1, source_target_pairs={{0,12},{2,14},{4,8},{6,10},{8,4},{10,6},{12,0},{14,2},{1,13},{3,15... | collective-permute-start | bytes 399368 | tf_op jit(solution)/shard_map/ppermute | solution.py:538
  17.6 0.0 copy-done
  17.6 25.5 %tail_attention.1.out_in = bf16[1,272,32,128]{3,2,1,0:T(8,128)(2,1)} custom-call(s32[1]{0:T(128)S(6)} %copy.13.prefix_ref, bf16[1,272,32,128]{3,2,1,0:T(8,128)(2,1)S(1)} %copy-done, bf16[4,1280,128]{2,1,0:T(8,128)(2,1)S(1)} %get-tuple-element.31.keys, bf16[4,144,1280]{2,1,0:T(8,128)(2,1)S(1)} %get-tuple-element.32.values_t), custom_call_target="tpu_custom_call" | custom-call | flops 21474836480 | bytes 8388608 | tf_op jit(solution)/shard_map/tail_attention/pallas_call | solution.py:320
  43.1 0.0 collective-permute-done.2.refs_2_
  43.1 0.0 collective-permute-done.3.refs_3_
  43.1 0.0 collective-permute-done.4.refs_5_
  43.1 0.0 collective-permute-done.5.refs_6_
  43.2 0.0 collective-permute-done.6.refs_7_
  43.2 2.7 %decode_pages.1 = bf16[1,272,32,128]{3,2,1,0:T(8,128)(2,1)} custom-call(bf16[4,128,256]{2,1,0:T(8,128)(2,1)S(1)} %get-tuple-element.23.scaled_ref, f32[4,128,128]{2,1,0:T(8,128)S(1)} %get-tuple-element.24.m_in, f32[4,128,128]{2,1,0:T(8,128)S(1)} %get-tuple-element.25.l_in, ...), custom_call_target="tpu_custom_call", output_to_operand_aliasing={{}: (4, {})} | custom-call | tf_op jit(solution)/shard_map/decode_pages/pallas_call | solution.py:483
Async XLA Ops:
  1.3 13.6 %collective-permute-start = (bf16[520,128]{1,0:T(8,128)(2,1)S(1)}, bf16[520,128]{1,0:T(8,128)(2,1)S(1)}, u32[]{:S(2)}, u32[]{:S(2)}) collective-permute-start(bf16[520,128]{1,0:T(8,128)(2,1)S(1)} %get-tuple-element.28), channel_id=1, source_target_pairs={{0,8},{2,10},{4,12},{6,14},{8,0},{10,2},{12,4},{14,6},{1,9},{3,11}... | collective-permute-start | bytes 399368 | tf_op jit(solution)/shard_map/ppermute | solution.py:538
  5.4 11.2 %collective-permute-start.1 = (bf16[520,128]{1,0:T(8,128)(2,1)S(1)}, bf16[520,128]{1,0:T(8,128)(2,1)S(1)}, u32[]{:S(2)}, u32[]{:S(2)}) collective-permute-start(bf16[520,128]{1,0:T(8,128)(2,1)S(1)} %get-tuple-element.34), channel_id=1, source_target_pairs={{0,2},{2,0},{4,6},{6,4},{8,10},{10,8},{12,14},{14,12},{1,3},{3,1},... | collective-permute-start | bytes 399368 | tf_op jit(solution)/shard_map/ppermute | solution.py:538
  7.0 36.2 %collective-permute-start.2 = (bf16[520,128]{1,0:T(8,128)(2,1)S(1)}, bf16[520,128]{1,0:T(8,128)(2,1)S(1)}, u32[]{:S(2)}, u32[]{:S(2)}) collective-permute-start(bf16[520,128]{1,0:T(8,128)(2,1)S(1)} %get-tuple-element.35), channel_id=1, source_target_pairs={{0,4},{2,6},{4,0},{6,2},{8,12},{10,14},{12,8},{14,10},{1,5},{3,7},... | collective-permute-start | bytes 399368 | tf_op jit(solution)/shard_map/ppermute | solution.py:538
  8.5 34.6 %collective-permute-start.3 = (bf16[520,128]{1,0:T(8,128)(2,1)S(1)}, bf16[520,128]{1,0:T(8,128)(2,1)S(1)}, u32[]{:S(2)}, u32[]{:S(2)}) collective-permute-start(bf16[520,128]{1,0:T(8,128)(2,1)S(1)} %get-tuple-element.36), channel_id=1, source_target_pairs={{0,6},{2,4},{4,2},{6,0},{8,14},{10,12},{12,10},{14,8},{1,7},{3,5},... | collective-permute-start | bytes 399368 | tf_op jit(solution)/shard_map/ppermute | solution.py:538
  8.9 34.2 %collective-permute-start.4 = (bf16[520,128]{1,0:T(8,128)(2,1)S(1)}, bf16[520,128]{1,0:T(8,128)(2,1)S(1)}, u32[]{:S(2)}, u32[]{:S(2)}) collective-permute-start(bf16[520,128]{1,0:T(8,128)(2,1)S(1)} %get-tuple-element.38), channel_id=1, source_target_pairs={{0,14},{2,12},{4,10},{6,8},{8,6},{10,4},{12,2},{14,0},{1,15},{3,13... | collective-permute-start | bytes 399368 | tf_op jit(solution)/shard_map/ppermute | solution.py:538
  11.9 5.7 %copy-start = (bf16[1,272,32,128]{3,2,1,0:T(8,128)(2,1)S(1)}, bf16[1,272,32,128]{3,2,1,0:T(8,128)(2,1)}, u32[]{:S(2)}) copy-start(bf16[1,272,32,128]{3,2,1,0:T(8,128)(2,1)} %q_ref.1) | copy-start | bytes 6684676
  14.9 28.2 %collective-permute-start.5 = (bf16[520,128]{1,0:T(8,128)(2,1)S(1)}, bf16[520,128]{1,0:T(8,128)(2,1)S(1)}, u32[]{:S(2)}, u32[]{:S(2)}) collective-permute-start(bf16[520,128]{1,0:T(8,128)(2,1)S(1)} %get-tuple-element.39), channel_id=1, source_target_pairs={{0,10},{2,8},{4,14},{6,12},{8,2},{10,0},{12,6},{14,4},{1,11},{3,9}... | collective-permute-start | bytes 399368 | tf_op jit(solution)/shard_map/ppermute | solution.py:538
  16.6 26.5 %collective-permute-start.6 = (bf16[520,128]{1,0:T(8,128)(2,1)S(1)}, bf16[520,128]{1,0:T(8,128)(2,1)S(1)}, u32[]{:S(2)}, u32[]{:S(2)}) collective-permute-start(bf16[520,128]{1,0:T(8,128)(2,1)S(1)} %get-tuple-element.40), channel_id=1, source_target_pairs={{0,12},{2,14},{4,8},{6,10},{8,4},{10,6},{12,0},{14,2},{1,13},{3,15... | collective-permute-start | bytes 399368 | tf_op jit(solution)/shard_map/ppermute | solution.py:538
